TPU v7x, 32 devices: a whole 2x2x4 slice. The times are simulated.
32 devices in a mesh: vol: 16 (over z, y, x), path: 2 (over core).
Axes of the slice: x: 2, y: 2, z: 4, core: 2. Of those that a mesh axis runs over, the one named last changes fastest.
Arguments:
- factors: bfloat16 [16, 2048], P(None, 'path'), may hold values from -6 to 6
- payoff: float32 [4, 2048], P(None, 'path'), may hold values from -6 to 6
- terminal: float32 [16, 2048], P('vol', 'path'), may hold values from 0.5 to 4
- decisions: int32 [3, 16, 2048], P(None, 'vol', 'path'), may hold values 0 or 1
- level_range: int32 [4, 2], replicated, may hold values from 1 to 15, as said below
- w_in_master: float32 [16, 16, 1024], P('vol'), may hold values from -1.5 to 1.5
- w_mid_master: float32 [16, 1024, 1024], P('vol', 'path'), may hold values from -0.1875 to 0.1875
- vec_master: float32 [16, 3, 1024], P('vol'), may hold values from -0.6 to 0.6
- w_in_copy: bfloat16 [16, 16, 1024], P('vol'), may hold values from -1.5 to 1.5
- w_mid_copy: bfloat16 [16, 1024, 1024], P('vol', 'path'), may hold values from -0.1875 to 0.1875
- mom_in: float32 [16, 16, 1024], P('vol'), may hold values from -0.6 to 0.6
- mom_mid: float32 [16, 1024, 1024], P('vol', 'path'), may hold values from -0.6 to 0.6
- mom_vec: float32 [16, 3, 1024], P('vol'), may hold values from -0.6 to 0.6
Outputs:
- level_value: float32 [16], P('vol')
- new_w_in: float32 [16, 16, 1024], P('vol')
- new_w_mid: float32 [16, 1024, 1024], P('vol', 'path')
- new_vec: float32 [16, 3, 1024], P('vol')
- new_mom_in: float32 [16, 16, 1024], P('vol')
- new_mom_mid: float32 [16, 1024, 1024], P('vol', 'path')
- new_mom_vec: float32 [16, 3, 1024], P('vol')
- new_in_copy: bfloat16 [16, 16, 1024], P('vol')
- new_mid_copy: bfloat16 [16, 1024, 1024], P('vol', 'path')
Inputs may be any that keep to these rules, and one draw needn't show every extreme that they name: At every date level_range[s, 0] <= level_range[s, 1] and level 0 lies below the range; at dates 1 to 3 the range starts at level 1; at date 0 the range holds exactly 8 levels.
All inputs are finite; a program needn't handle non-finite values. No bound on the sum of `decisions` on one device may be relied on, other than what follows from the above.
Results may differ from a plain program's by a relative error of at most 0.015.
Values may be sent and summed in bfloat16 or wider, within the bound.
No kernel may reach another device: no remote copies, remote signals or barrier semaphores. Data moves between devices by JAX's collectives and lax.ppermute only.
A program may use at most 64 MiB of HBM per device.

v0:
```python
import jax
import jax.numpy as jnp
from jax import lax
from jax.sharding import PartitionSpec as P

MOMENTUM = 0.9
STEP_SIZE = 0.01


def from_behind(value, axis, steps):
    count = lax.axis_size(axis)
    leading, last = (max(0, -steps), min(count, count - steps))
    return lax.ppermute(value, axis, [(source, source + steps) for source in range(leading, last)])


def silu_parts(preact):
    squash = jax.nn.sigmoid(preact)
    return (preact * squash, squash * (1.0 + preact * (1.0 - squash)))


def network_pass(w_first, w_second, vectors, features, gain_row, enabled):
    pre_one = (
        lax.dot_general(
            features, w_first, (((0,), (0,)), ((), ())), preferred_element_type=jnp.float32
        )
        + vectors[0]
    )
    act_one, slope_one = silu_parts(pre_one)
    hidden_one = act_one.astype(jnp.bfloat16)
    pre_two = jnp.dot(hidden_one, w_second, preferred_element_type=jnp.float32) + vectors[1]
    act_two, slope_two = silu_parts(pre_two)
    hidden_two = act_two.astype(jnp.bfloat16)
    logits = jnp.sum(hidden_two.astype(jnp.float32) * vectors[2], axis=1)
    chance = jax.nn.sigmoid(logits)
    d_logit = jnp.where(enabled, -gain_row * chance * (1.0 - chance), 0.0)
    d_head = jnp.sum(d_logit[:, None] * hidden_two.astype(jnp.float32), axis=0)
    d_pre_two = d_logit[:, None] * vectors[2] * slope_two
    d_bias_two = jnp.sum(d_pre_two, axis=0)
    d_two_low = d_pre_two.astype(jnp.bfloat16)
    d_hidden_one = lax.dot_general(
        d_two_low, w_second, (((1,), (1,)), ((), ())), preferred_element_type=jnp.float32
    )
    d_pre_one = d_hidden_one * slope_one
    d_bias_one = jnp.sum(d_pre_one, axis=0)
    d_first = jnp.dot(features, d_pre_one.astype(jnp.bfloat16), preferred_element_type=jnp.float32)
    d_vectors = jnp.stack([d_bias_one, d_bias_two, d_head])
    value_sum = jnp.where(enabled, jnp.sum(chance * gain_row), 0.0)
    return (hidden_one, d_two_low, d_first, d_vectors, value_sum)


def row_product(hidden_one, d_two_low):
    return lax.dot_general(
        hidden_one, d_two_low, (((0,), (0,)), ((), ())), preferred_element_type=jnp.float32
    )


def lower_neighbour(values):
    return from_behind(values, "vol", 1)


def full_rows(row_shard):
    return lax.all_gather(row_shard, "path", axis=0, tiled=True)


def shards(
    factors,
    payoff,
    terminal,
    decisions,
    level_range,
    w_in_master,
    w_mid_master,
    vec_master,
    w_in_copy,
    w_mid_copy,
    mom_in,
    mom_mid,
    mom_vec,
):
    level_here = lax.axis_index("vol")
    dates = payoff.shape[0]
    paths_here = payoff.shape[1]
    carry_value = terminal[0]
    for date_index in range(dates - 1, 0, -1):
        lower_row = lower_neighbour(carry_value)
        lower_end = level_range[date_index, 0]
        upper_end = level_range[date_index, 1]
        inside = jnp.logical_and(level_here >= lower_end, level_here <= upper_end)
        taken_now = jnp.where(
            level_here > upper_end,
            1.0,
            jnp.where(inside, decisions[date_index - 1, 0].astype(jnp.float32), 0.0),
        )
        carry_value = taken_now * (payoff[date_index] + lower_row) + (1.0 - taken_now) * carry_value
    lower_row = lower_neighbour(carry_value)
    gain_row = payoff[0] + lower_row - carry_value
    low_now = level_range[0, 0]
    high_now = level_range[0, 1]
    active = jnp.logical_and(level_here >= low_now, level_here <= high_now)
    forced = jnp.where(level_here > high_now, 1.0, 0.0)
    first_copy = w_in_copy[0]
    vectors = vec_master[0]
    second_full = full_rows(w_mid_copy[0])
    hidden_one, d_two_low, d_first, d_vectors, value_sum = network_pass(
        first_copy, second_full, vectors, factors, gain_row, active
    )
    mid_grad = lax.psum_scatter(
        row_product(hidden_one, d_two_low).astype(jnp.bfloat16),
        "path",
        scatter_dimension=0,
        tiled=True,
    ).astype(jnp.float32)
    value_local = jnp.where(active, value_sum, forced * jnp.sum(gain_row)) + jnp.sum(carry_value)
    d_first, d_vectors, value_local = lax.psum((d_first, d_vectors, value_local), "path")
    paths_total = paths_here * lax.axis_size("path")
    level_value = (value_local / paths_total)[None]
    new_mom_in = MOMENTUM * mom_in + d_first[None]
    new_mom_mid = MOMENTUM * mom_mid + mid_grad[None]
    new_mom_vec = MOMENTUM * mom_vec + d_vectors[None]
    new_w_in = w_in_master - STEP_SIZE * new_mom_in
    new_w_mid = w_mid_master - STEP_SIZE * new_mom_mid
    new_vec = vec_master - STEP_SIZE * new_mom_vec
    return (
        level_value,
        new_w_in,
        new_w_mid,
        new_vec,
        new_mom_in,
        new_mom_mid,
        new_mom_vec,
        new_w_in.astype(jnp.bfloat16),
        new_w_mid.astype(jnp.bfloat16),
    )


def solution(mesh):
    in_specs = (
        P(None, "path"),
        P(None, "path"),
        P("vol", "path"),
        P(None, "vol", "path"),
        P(),
        P("vol", None, None),
        P("vol", "path", None),
        P("vol", None, None),
        P("vol", None, None),
        P("vol", "path", None),
        P("vol", None, None),
        P("vol", "path", None),
        P("vol", None, None),
    )
    out_specs = (
        P("vol"),
        P("vol", None, None),
        P("vol", "path", None),
        P("vol", None, None),
        P("vol", None, None),
        P("vol", "path", None),
        P("vol", None, None),
        P("vol", None, None),
        P("vol", "path", None),
    )
    return jax.shard_map(shards, mesh=mesh, in_specs=in_specs, out_specs=out_specs, check_vma=False)
```

profile of v0, /device:TPU:0, one launch (start us, length us, event | category | flops | bytes accessed | tf_op | source)
XLA Modules:
  0.0 99.6 jit_solution(18140826427219858401)
XLA Ops:
  7.2 0.0 copy-start
  7.2 0.0 all-gather.3.cloned.1.call-start
  7.2 0.7 all-gather.3.cloned.1.call-update
  7.9 0.0 all-reduce.3.cloned.1.call-start
  8.0 4.8 %collective-permute-start = (f32[1024]{0:T(1024)}, f32[1024]{0:T(1024)S(1)}, u32[]{:S(2)}, u32[]{:S(2)}) collective-permute-start(f32[1024]{0:T(1024)} %bitcast.63), channel_id=1, source_target_pairs={{0,2},{2,4},{4,6},{6,8},{8,10},{10,12},{12,14},{14,16},{16,18},{18... | collective-permute-start | bytes 12296 | tf_op jit(solution)/shard_map/ppermute | solution.py:13
  12.8 1.6 %fusion.21 = (s32[1,1]{0,1:T(1,128)}, s32[1,1]{0,1:T(1,128)}, s32[1,1]{0,1:T(1,128)}, s32[1,1]{0,1:T(1,128)}, s32[1,1]{0,1:T(1,128)}, /*index=5*/s32[1,1]{0,1:T(1,128)}, s32[1,1]{0,1:T(1,128)}, s32[1,1]{0,1:T(1,128)}) fusion(s32[4,2]{0,1:T(2,128)} %param.17), kind=kLoop, calls=%fused_computation.48 | loop fusion | bytes 64 | tf_op jit(solution)/shard_map/slice | solution.py:86
  20.3 0.9 fusion.19
  21.2 0.7 broadcast_select_fusion.5
  21.9 0.0 collective-permute-done
  21.9 0.7 multiply_add_fusion.4
  22.6 3.4 %collective-permute-start.1 = (f32[1024]{0:T(1024)S(1)}, f32[1024]{0:T(1024)S(1)}, u32[]{:S(2)}, u32[]{:S(2)}) collective-permute-start(f32[1024]{0:T(1024)S(1)} %multiply_add_fusion.4), channel_id=1, source_target_pairs={{0,2},{2,4},{4,6},{6,8},{8,10},{10,12},{12,14},{14,16},{16,18},{18... | collective-permute-start | bytes 12296 | tf_op jit(solution)/shard_map/ppermute | solution.py:13
  26.0 3.5 %fusion.12 = f32[1024,1024]{1,0:T(8,128)} fusion(bf16[16,1024]{1,0:T(8,128)(2,1)S(1)} %copy-done, bf16[1,16,1024]{2,1,0:T(8,128)(2,1)} %param.21), kind=kOutput, calls=%fused_computation.23 | convolution fusion | flops 33554432 | bytes 4259840 | tf_op jit(solution)/shard_map/dot_general | solution.py:23
  29.5 3.4 %collective-permute-start.2 = (f32[1024]{0:T(1024)S(1)}, f32[1024]{0:T(1024)S(1)}, u32[]{:S(2)}, u32[]{:S(2)}) collective-permute-start(f32[1024]{0:T(1024)S(1)} %multiply_add_fusion.3), channel_id=1, source_target_pairs={{0,2},{2,4},{4,6},{6,8},{8,10},{10,12},{12,14},{14,16},{16,18},{18... | collective-permute-start | bytes 12296 | tf_op jit(solution)/shard_map/ppermute | solution.py:13
  34.2 0.0 collective-permute-done.2
  34.2 0.6 fusion.18
  34.8 4.1 %collective-permute-start.3 = (f32[1024]{0:T(1024)S(1)}, f32[1024]{0:T(1024)S(1)}, u32[]{:S(2)}, u32[]{:S(2)}) collective-permute-start(f32[1024]{0:T(1024)S(1)} %get-tuple-element.26), channel_id=1, source_target_pairs={{0,2},{2,4},{4,6},{6,8},{8,10},{10,12},{12,14},{14,16},{16,18},{18... | collective-permute-start | bytes 12296 | tf_op jit(solution)/shard_map/ppermute | solution.py:13
  39.0 0.0 all-gather.3.cloned.1.call-done
  39.0 7.4 %fusion = (f32[1024]{0:T(1024)S(1)}, bf16[1024,1024]{1,0:T(8,128)(2,1)}, f32[1024,1024]{1,0:T(8,128)S(1)}) fusion(f32[1024]{0:T(1024)S(1)} %bitcast.59, f32[1024]{0:T(1024)S(1)} %bitcast.55, bf16[1,1024,1024]{2,1,0:T(8,128)(2,1)} %all-gather.3.cloned.1.call-done, f32[1024,1024]{1,0:T(8,128)} %fusion.12, f32[1024]{0:T(1024)S(1)} %bitcast.66), kind=kOutput, calls=%fused_computation.2 | convolution fusion | flops 2163211264 | bytes 12599296 | tf_op jit(solution)/shard_map/dot_general | solution.py:30
  46.5 0.0 collective-permute-done.3
  46.5 5.3 %fusion.22 = (f32[1024]{0:T(1024)S(1)}, bf16[1024,1024]{1,0:T(8,128)(2,1)S(1)}) fusion(f32[1024,1024]{1,0:T(8,128)S(1)} %copy-done.1, f32[1024]{0:T(1024)S(1)} %bitcast.67, bf16[1,1024,1024]{2,1,0:T(8,128)(2,1)S(1)} %copy-done.8, f32[1024,1024]{1,0:T(8,128)S(1)} %get-tuple-element.47, f32[1024]{0:T(1024)S(1)} %bitcast.56, f32[1024]{0:T(1024)S(1)} %bitcast.60, ...), kind=kOutput, calls=%fused_computation.49 | convolution fusion | flops 2170551296 | bytes 12603392 | tf_op jit(solution)/shard_map/dot_general | solution.py:40
  51.8 1.0 %fusion.7 = f32[1,16,1024]{2,1,0:T(8,128)} fusion(bf16[16,1024]{1,0:T(8,128)(2,1)S(1)} %copy-done, bf16[1024,1024]{1,0:T(8,128)(2,1)S(1)} %get-tuple-element.49), kind=kOutput, calls=%fused_computation.18 | convolution fusion | flops 33554432 | bytes 2195456 | tf_op jit(solution)/shard_map/dot_general | solution.py:45
  52.9 0.0 all-reduce.3.cloned.1.call-update
  52.9 0.0 reduce-scatter.2.cloned.1.call-start
  52.9 8.6 %convolution_convert_fusion = bf16[1024,1024]{1,0:T(8,128)(2,1)} fusion(f32[1024,1024]{1,0:T(8,128)} %fusion.12, f32[1024]{0:T(1024)S(1)} %bitcast.68, f32[1024,1024]{1,0:T(8,128)} %copy-done.2, f32[1024]{0:T(1024)S(1)} %get-tuple-element.23, f32[1024]{0:T(1024)S(1)} %bitcast.61, f32[1024]{0:T(1024)S(1)} %bitcast.57), kind=kOutput, calls=%fused_computation.17 | convolution fusion | flops 2166358016 | bytes 10502144 | tf_op jit(solution)/shard_map/dot_general | solution.py:52
  61.6 0.0 reduce-scatter.2.cloned.1.call-update
  62.4 0.6 fusion.15
  63.7 4.2 %fusion.14 = (f32[1024]{0:T(1024)S(1)}, f32[1024]{0:T(1024)S(1)}) fusion(f32[1024,1024]{1,0:T(8,128)} %copy-done.2, f32[1024]{0:T(1024)S(1)} %bitcast.58, f32[1024]{0:T(1024)S(1)} %bitcast.62, f32[1024]{0:T(1024)S(1)} %get-tuple-element.23, bf16[1024,1024]{1,0:T(8,128)(2,1)} %get-tuple-element.28), kind=kLoop, calls=%fused_computation.41 | loop fusion | flops 14678016 | bytes 6311936 | tf_op jit(solution)/shard_map/reduce_sum | solution.py:38
  69.2 3.9 %all-reduce = (f32[]{:T(128)}, f32[1,3,1024]{2,0,1:T(1,128)S(1)}) all-reduce(f32[]{:T(128)S(6)} %add.92, f32[1,3,1024]{2,0,1:T(1,128)S(1)} %broadcast_in_dim.36), channel_id=1, replica_groups=mesh['vol'=16,'path'=2] {'path'}, use_global_device_ids=true, to_apply=%region_4.5 | all-reduce | flops 3073 | bytes 24584 | tf_op jit(solution)/shard_map/psum | solution.py:114
  73.8 0.6 multiply_subtract_fusion.2
  74.4 1.5 %fusion.17 = (bf16[1,16,1024]{2,1,0:T(8,128)(2,1)}, f32[1,16,1024]{2,1,0:T(8,128)}, f32[1,16,1024]{2,1,0:T(8,128)}) fusion(f32[1,16,1024]{2,1,0:T(8,128)S(1)} %copy-done.4, f32[1,16,1024]{2,1,0:T(8,128)} %all-reduce.3.cloned.1.call-done, f32[1,16,1024]{2,1,0:T(8,128)S(1)} %copy-done.5), kind=kLoop, calls=%fused_computation.44 | loop fusion | flops 81920 | bytes 360448 | tf_op jit(solution)/shard_map/convert_element_type | solution.py:131
  75.9 10.9 %reduce-scatter.2.cloned.1.call-done = bf16[512,1024]{1,0:T(8,128)(2,1)} async-done(((bf16[1024,1024]{1,0:T(8,128)(2,1)}), bf16[512,1024]{1,0:T(8,128)(2,1)}) %reduce-scatter.2.cloned.1.call-update) | async-done | bytes 1048592 | tf_op jit(solution)/shard_map/reduce_scatter | solution.py:107
  86.8 5.1 %fusion.16 = (bf16[1,512,1024]{2,1,0:T(8,128)(2,1)}, f32[1,512,1024]{2,1,0:T(8,128)}, f32[1,512,1024]{2,1,0:T(8,128)}) fusion(f32[1,512,1024]{2,1,0:T(8,128)S(1)} %copy-done.3, bf16[512,1024]{1,0:T(8,128)(2,1)} %reduce-scatter.2.cloned.1.call-done, f32[1,512,1024]{2,1,0:T(8,128)} %param.24), kind=kLoop, calls=%fused_computation.43 | loop fusion | flops 3145728 | bytes 10485760 | tf_op jit(solution)/shard_map/convert_element_type | solution.py:132
  (24 shorter events, 0.1 us)
Async XLA Ops:
  7.2 18.8 %copy-start = (bf16[16,1024]{1,0:T(8,128)(2,1)S(1)}, bf16[16,1024]{1,0:T(8,128)(2,1)}, u32[]{:S(2)}) copy-start(bf16[16,1024]{1,0:T(8,128)(2,1)} %param.13) | copy-start | bytes 98308
  7.2 25.7 %copy-start.6 = (f32[1,3,1024]{2,0,1:T(1,128)S(1)}, f32[1,3,1024]{2,0,1:T(1,128)}, u32[]{:S(2)}) copy-start(f32[1,3,1024]{2,0,1:T(1,128)} %param.20) | copy-start | bytes 36868
  7.2 31.8 %all-gather.3.cloned.1.call-start = ((), (), s32[]{:S(2)}) async-start(), calls=%async_computation.3 | async-start | bytes 3145728 | tf_op jit(solution)/shard_map/all_gather | solution.py:62
  7.9 66.5 %all-reduce.3.cloned.1.call-start = ((), (), s32[]{:S(2)}) async-start(), calls=%async_computation.1 | async-start | bytes 131072 | tf_op jit(solution)/shard_map/psum | solution.py:114
  8.0 13.9 %collective-permute-start = (f32[1024]{0:T(1024)}, f32[1024]{0:T(1024)S(1)}, u32[]{:S(2)}, u32[]{:S(2)}) collective-permute-start(f32[1024]{0:T(1024)} %bitcast.63), channel_id=1, source_target_pairs={{0,2},{2,4},{4,6},{6,8},{8,10},{10,12},{12,14},{14,16},{16,18},{18... | collective-permute-start | bytes 12296 | tf_op jit(solution)/shard_map/ppermute | solution.py:13
  22.6 6.9 %collective-permute-start.1 = (f32[1024]{0:T(1024)S(1)}, f32[1024]{0:T(1024)S(1)}, u32[]{:S(2)}, u32[]{:S(2)}) collective-permute-start(f32[1024]{0:T(1024)S(1)} %multiply_add_fusion.4), channel_id=1, source_target_pairs={{0,2},{2,4},{4,6},{6,8},{8,10},{10,12},{12,14},{14,16},{16,18},{18... | collective-permute-start | bytes 12296 | tf_op jit(solution)/shard_map/ppermute | solution.py:13
  29.5 4.7 %collective-permute-start.2 = (f32[1024]{0:T(1024)S(1)}, f32[1024]{0:T(1024)S(1)}, u32[]{:S(2)}, u32[]{:S(2)}) collective-permute-start(f32[1024]{0:T(1024)S(1)} %multiply_add_fusion.3), channel_id=1, source_target_pairs={{0,2},{2,4},{4,6},{6,8},{8,10},{10,12},{12,14},{14,16},{16,18},{18... | collective-permute-start | bytes 12296 | tf_op jit(solution)/shard_map/ppermute | solution.py:13
  34.8 11.6 %collective-permute-start.3 = (f32[1024]{0:T(1024)S(1)}, f32[1024]{0:T(1024)S(1)}, u32[]{:S(2)}, u32[]{:S(2)}) collective-permute-start(f32[1024]{0:T(1024)S(1)} %get-tuple-element.26), channel_id=1, source_target_pairs={{0,2},{2,4},{4,6},{6,8},{8,10},{10,12},{12,14},{14,16},{16,18},{18... | collective-permute-start | bytes 12296 | tf_op jit(solution)/shard_map/ppermute | solution.py:13
  39.0 7.5 %copy-start.1 = (f32[1024,1024]{1,0:T(8,128)S(1)}, f32[1024,1024]{1,0:T(8,128)}, u32[]{:S(2)}) copy-start(f32[1024,1024]{1,0:T(8,128)} %fusion.12) | copy-start | bytes 12582916
  39.0 7.5 %copy-start.8 = (bf16[1,1024,1024]{2,1,0:T(8,128)(2,1)S(1)}, bf16[1,1024,1024]{2,1,0:T(8,128)(2,1)}, u32[]{:S(2)}) copy-start(bf16[1,1024,1024]{2,1,0:T(8,128)(2,1)} %all-gather.3.cloned.1.call-done) | copy-start | bytes 6291460
  46.5 5.4 %copy-start.2 = (f32[1024,1024]{1,0:T(8,128)}, f32[1024,1024]{1,0:T(8,128)S(1)}, u32[]{:S(2)}) copy-start(f32[1024,1024]{1,0:T(8,128)S(1)} %get-tuple-element.47) | copy-start | bytes 12582916
  52.9 33.9 %reduce-scatter.2.cloned.1.call-start = ((), (), s32[]{:S(2)}) async-start(), calls=%async_computation.2 | async-start | bytes 3145728 | tf_op jit(solution)/shard_map/reduce_scatter | solution.py:107
  61.6 12.2 %copy-start.7 = (f32[1,3,1024]{2,0,1:T(1,128)S(1)}, f32[1,3,1024]{2,0,1:T(1,128)}, u32[]{:S(2)}) copy-start(f32[1,3,1024]{2,0,1:T(1,128)} %param.25) | copy-start | bytes 36868
  61.6 12.9 %copy-start.4 = (f32[1,16,1024]{2,1,0:T(8,128)S(1)}, f32[1,16,1024]{2,1,0:T(8,128)}, u32[]{:S(2)}) copy-start(f32[1,16,1024]{2,1,0:T(8,128)} %param.18) | copy-start | bytes 196612
  61.6 12.9 %copy-start.5 = (f32[1,16,1024]{2,1,0:T(8,128)S(1)}, f32[1,16,1024]{2,1,0:T(8,128)}, u32[]{:S(2)}) copy-start(f32[1,16,1024]{2,1,0:T(8,128)} %param.23) | copy-start | bytes 196612
  61.6 25.3 %copy-start.3 = (f32[1,512,1024]{2,1,0:T(8,128)S(1)}, f32[1,512,1024]{2,1,0:T(8,128)}, u32[]{:S(2)}) copy-start(f32[1,512,1024]{2,1,0:T(8,128)} %param.19) | copy-start | bytes 6291460
Sparse Core Ops, SparseCore 0:
  9.6 13.2 all-gather.2
  53.0 20.1 all-reduce.2
  76.0 10.7 reduce-scatter.1
where the time goes:
time: 100 us; the launch traced here: 99.6 us
  matrix products  25.9 us (26%)
  between operations  25.7 us (26%)
  starting transfers between devices  15.9 us (16%)
  other arithmetic  14.2 us (14%)
  waiting for transfers between devices  11.6 us (12%)
  blocking collectives  3.87 us (4%)
  local copies, waits for them, and re-layouts  2.52 us (3%)
    ppermute x4, starting transfers between devices, from_behind(): lax.ppermute(value, axis, [(source, source + steps) for source in range(l...  15.8 us
    reduce_scatter x1, waiting for transfers between devices, shards(): lax.psum_scatter(row_product(hidden_one, d_two_low).astype(jnp.bfloat16),...  10.9 us
    dot_general x1, matrix products, row_product(): lax.dot_general(hidden_one, d_two_low, (((0,), (0,)), ((), ())), preferre...  8.62 us
    dot_general x1, matrix products, network_pass(): jnp.dot(hidden_one, w_second, preferred_element_type=jnp.float32)  7.42 us
    dot_general x1, matrix products, network_pass(): lax.dot_general(d_two_low, w_second, (((1,), (1,)), ((), ())), preferred_...  5.33 us
    convert_element_type x1, other arithmetic, shards(): new_w_mid.astype(jnp.bfloat16)  5.11 us
    reduce_sum x1, other arithmetic, network_pass(): d_bias_two = jnp.sum(d_pre_two, axis=0)  4.22 us
    psum x1, blocking collectives, shards(): lax.psum((d_first, d_vectors, value_local), 'path')  3.87 us
  transfers between devices with their start and end apart: 7, of which 1 were waited for; matrix products, arithmetic and copies ran while one was open for 31% of the time, Pallas kernels for 0%

commit v1 on v0

v1 whole, which is shorter than its diff:
```python
import jax
import jax.numpy as jnp
from jax import lax
from jax.experimental import pallas as pl
from jax.experimental.pallas import tpu as pltpu
from jax.sharding import PartitionSpec as P

MOMENTUM = 0.9
STEP_SIZE = 0.01
LOWER_LEVELS = 4
SMALL_ROWS = 24
VMEM_LIMIT = 30 * 1024 * 1024


def vmem_specs(count):
    return [pl.BlockSpec(memory_space=pltpu.VMEM)] * count


def call(kernel, out_shape, in_specs, name, flops, scratch=(), **options):
    return pl.pallas_call(
        kernel,
        out_shape=out_shape,
        in_specs=in_specs,
        out_specs=jax.tree.map(lambda _: pl.BlockSpec(memory_space=pltpu.VMEM), out_shape),
        scratch_shapes=list(scratch),
        compiler_params=pltpu.CompilerParams(vmem_limit_bytes=VMEM_LIMIT, **options),
        cost_estimate=pl.CostEstimate(flops=flops, bytes_accessed=1 << 20, transcendentals=0),
        name=name,
    )


def half_columns(flip, half, width):
    return pl.ds(pl.multiple_of((flip ^ half) * width, width), width)


def silu_parts(preact):
    squash = 0.5 + 0.5 * jnp.tanh(0.5 * preact)
    act = preact * squash
    return act, squash + act * (1.0 - squash)


def first_layer(flip_of, factors, w_in, vectors, hidden_one, slope_one):
    flip = flip_of()
    hidden = w_in.shape[1]
    width, paths, tile, rows = hidden // 2, factors.shape[1], 128, 32
    for half in range(2):
        columns = half_columns(flip, half, width)
        weights = w_in[:, columns]
        bias = vectors[0, :, columns]
        place = slice(half * width, (half + 1) * width)
        for start in range(0, paths, tile):
            pre = lax.dot_general(
                factors[:, start : start + tile],
                weights,
                (((0,), (0,)), ((), ())),
                preferred_element_type=jnp.float32,
            )
            for row in range(0, tile, rows):
                act, slope = silu_parts(pre[row : row + rows] + bias)
                here = slice(start + row, start + row + rows)
                hidden_one[here, place] = act.astype(jnp.bfloat16)
                slope_one[here, place] = slope.astype(jnp.bfloat16)


def continuation(level, level_range, payoff, row_sets):
    dates = payoff.shape[0]
    conts = [
        jnp.where(level >= below, rows[0:1, :], 0.0) for below, rows in enumerate(row_sets)
    ]
    for date in range(dates - 1, 0, -1):
        low, high = level_range[0, date], level_range[1, date]
        updated = []
        for below in range(len(conts) - 1):
            here = level - below
            chosen = row_sets[below][dates - date : dates - date + 1, :]
            inside = jnp.logical_and(here >= low, here <= high)
            taken = jnp.where(here > high, 1.0, jnp.where(inside, chosen, 0.0))
            value = taken * (payoff[date : date + 1, :] + conts[below + 1]) + (1.0 - taken) * conts[below]
            updated.append(jnp.where(here >= 0, value, 0.0))
        conts = updated
    return conts


def second_layer(
    hidden_one, w_own, w_other, vectors, level_range, payoff, own, low1, low2, low3, low4,
    d_two, grad_other, sums, gain_column, weighted_slope, act_two,
):
    level = lax.axis_index("vol")
    paths, hidden = hidden_one.shape
    width, tile, rows = hidden // 2, 128, 16
    row_sets = [ref[...] for ref in (own, low1, low2, low3, low4)]
    cont_here, cont_below = continuation(level, level_range, payoff, row_sets)
    gain = payoff[0:1, :] + cont_below - cont_here
    gain_column[...] = jnp.transpose(jnp.broadcast_to(gain, (8, paths)))
    low_now, high_now = level_range[0, 0], level_range[1, 0]
    active = jnp.logical_and(level >= low_now, level <= high_now)
    enabled = jnp.where(active, 1.0, 0.0)
    forced = jnp.where(level > high_now, 1.0, 0.0)
    bias, head = vectors[1], vectors[2]
    bias_sum = jnp.zeros((8, hidden), jnp.float32)
    head_sum = jnp.zeros((8, hidden), jnp.float32)
    value_sum = jnp.zeros((rows, 1), jnp.float32)
    for index, start in enumerate(range(0, paths, tile)):
        here = slice(start, start + tile)
        slot = index % 2
        pre = jnp.dot(hidden_one[here, :width], w_own[...], preferred_element_type=jnp.float32)
        pre += jnp.dot(hidden_one[here, width:], w_other[...], preferred_element_type=jnp.float32)
        d_logits = []
        for row in range(0, tile, rows):
            act, slope = silu_parts(pre[row : row + rows] + bias)
            act = act.astype(jnp.bfloat16).astype(jnp.float32)
            weighted_slope[slot, row : row + rows, :] = slope * head
            act_two[slot, row : row + rows, :] = act
            logits = jnp.sum(act * head, axis=1, keepdims=True)
            chance = 0.5 + 0.5 * jnp.tanh(0.5 * logits)
            gains = gain_column[start + row : start + row + rows, 0:1]
            d_logits.append(-enabled * gains * chance * (1.0 - chance))
            value_sum += chance * gains
        for row in range(0, tile, rows):
            d_logit = d_logits[row // rows]
            d_pre = d_logit * weighted_slope[slot, row : row + rows, :]
            scaled = d_logit * act_two[slot, row : row + rows, :]
            d_two[start + row : start + row + rows, :] = d_pre.astype(jnp.bfloat16)
            for part in range(0, rows, 8):
                bias_sum += d_pre[part : part + 8]
                head_sum += scaled[part : part + 8]
    chunk = 256
    for column in range(0, hidden, chunk):
        place = slice(column, column + chunk)
        grad_other[:, place] = lax.dot_general(
            hidden_one[:, width:],
            d_two[:, place],
            (((0,), (0,)), ((), ())),
            preferred_element_type=jnp.float32,
        ).astype(jnp.bfloat16)
    value_total = enabled * jnp.sum(value_sum) + forced * jnp.sum(gain) + jnp.sum(cont_here)
    sums[0:1, :] = jnp.sum(bias_sum, axis=0, keepdims=True)
    sums[1:2, :] = jnp.sum(head_sum, axis=0, keepdims=True)
    sums[2:3, :] = jnp.full((1, hidden), value_total, jnp.float32)
    sums[3:8, :] = jnp.zeros((5, hidden), jnp.float32)


def backward(flip_of, hidden_one, d_two, w_own, w_other, slope_one, factors, sums, grad_own, small, d_one):
    flip = flip_of()
    paths, hidden = hidden_one.shape
    width, tile, rows = hidden // 2, 128, 32
    count = factors.shape[0]
    bias_sums = [jnp.zeros((8, width), jnp.float32) for _ in range(2)]
    for start in range(0, paths, tile):
        for half, weights in enumerate((w_own, w_other)):
            place = slice(half * width, (half + 1) * width)
            d_hidden = lax.dot_general(
                d_two[start : start + tile, :],
                weights[...],
                (((1,), (1,)), ((), ())),
                preferred_element_type=jnp.float32,
            )
            for row in range(0, tile, rows):
                here = slice(start + row, start + row + rows)
                d_pre = d_hidden[row : row + rows] * slope_one[here, place].astype(jnp.float32)
                d_one[here, place] = d_pre.astype(jnp.bfloat16)
                for part in range(0, rows, 8):
                    bias_sums[half] += d_pre[part : part + 8]
    for half in range(2):
        columns = half_columns(flip, half, width)
        place = slice(half * width, (half + 1) * width)
        small[0:count, columns] = jnp.dot(
            factors[...], d_one[:, place], preferred_element_type=jnp.float32
        )
        small[count : count + 1, columns] = jnp.sum(bias_sums[half], axis=0, keepdims=True)
    small[count + 1 : count + 4, :] = sums[0:3, :]
    small[count + 4 : SMALL_ROWS, :] = jnp.zeros((SMALL_ROWS - count - 4, hidden), jnp.float32)
    chunk = 256
    for column in range(0, hidden, chunk):
        place = slice(column, column + chunk)
        grad_own[:, place] = lax.dot_general(
            hidden_one[:, :width],
            d_two[:, place],
            (((0,), (0,)), ((), ())),
            preferred_element_type=jnp.float32,
        )


def update(
    paths_total, grad_own, grad_other, small_own, small_other, mom_mid, w_mid, mom_in, w_in, mom_vec, vec,
    value, new_w_in, new_w_mid, new_vec, new_mom_in, new_mom_mid, new_mom_vec, new_in_copy, new_mid_copy,
):
    mom = MOMENTUM * mom_mid[...] + (grad_own[...] + grad_other[...].astype(jnp.float32))
    new_mom_mid[...] = mom
    master = w_mid[...] - STEP_SIZE * mom
    new_w_mid[...] = master
    new_mid_copy[...] = master.astype(jnp.bfloat16)

    @pl.when(pl.program_id(0) == 0)
    def _():
        small = small_own[...] + small_other[...]
        count = mom_in.shape[0]
        mom_first = MOMENTUM * mom_in[...] + small[:count]
        new_mom_in[...] = mom_first
        first = w_in[...] - STEP_SIZE * mom_first
        new_w_in[...] = first
        new_in_copy[...] = first.astype(jnp.bfloat16)
        for row in range(3):
            mom_row = MOMENTUM * mom_vec[row] + small[count + row : count + row + 1]
            new_mom_vec[row] = mom_row
            new_vec[row] = vec[row] - STEP_SIZE * mom_row
        value[0] = small[count + 3, 0] / paths_total


def step_of(mesh):
    levels, cores = mesh.shape["vol"], mesh.shape["path"]
    paired = cores == 2

    def flip_of():
        return lax.axis_index("path") if paired else 0

    def swap(value):
        return lax.ppermute(value, "path", [(0, 1), (1, 0)])

    def shards(
        factors, payoff, terminal, decisions, level_range, w_in_master, w_mid_master, vec_master,
        w_in_copy, w_mid_copy, mom_in, mom_mid, mom_vec,
    ):
        paths = factors.shape[1]
        count, hidden = w_in_copy.shape[1:]
        width = hidden // 2
        f32, bf16 = jnp.float32, jnp.bfloat16
        vectors = vec_master.transpose(1, 0, 2)
        if paired:
            w_own = w_mid_copy[0]
            w_other = swap(w_own)
        else:
            w_full = lax.all_gather(w_mid_copy[0], "path", axis=0, tiled=True)
            w_own, w_other = w_full[:width], w_full[width:]
        dates = payoff.shape[0]
        rows = jnp.concatenate(
            [terminal] + [decisions[date - 1].astype(f32) for date in range(dates - 1, 0, -1)]
        )
        lower = [
            lax.ppermute(rows, "vol", [(here, (here + below) % levels) for here in range(levels)])
            for below in range(1, LOWER_LEVELS + 1)
        ]
        square = 2 * paths * hidden * hidden
        hidden_one, slope_one = call(
            lambda *refs: first_layer(flip_of, *refs),
            (jax.ShapeDtypeStruct((paths, hidden), bf16),) * 2,
            vmem_specs(3),
            "first_layer",
            square,
        )(factors, w_in_copy[0], vectors)
        ranges = level_range.T
        d_two, grad_other, sums = call(
            second_layer,
            (
                jax.ShapeDtypeStruct((paths, hidden), bf16),
                jax.ShapeDtypeStruct((width, hidden), bf16),
                jax.ShapeDtypeStruct((8, hidden), f32),
            ),
            vmem_specs(4) + [pl.BlockSpec(memory_space=pltpu.SMEM)] + vmem_specs(6),
            "second_layer",
            2 * square,
            scratch=(
                pltpu.VMEM((paths, 8), f32),
                pltpu.VMEM((2, 128, hidden), f32),
                pltpu.VMEM((2, 128, hidden), f32),
            ),
        )(hidden_one, w_own, w_other, vectors, ranges, payoff, rows, *lower)
        if paired:
            grad_other = swap(grad_other)
        grad_own, small = call(
            lambda *refs: backward(flip_of, *refs),
            (
                jax.ShapeDtypeStruct((width, hidden), f32),
                jax.ShapeDtypeStruct((SMALL_ROWS, hidden), f32),
            ),
            vmem_specs(7),
            "backward",
            2 * square,
            scratch=(pltpu.VMEM((paths, hidden), bf16),),
        )(hidden_one, d_two, w_own, w_other, slope_one, factors, sums)
        if paired:
            small_other = swap(small)
        else:
            grads = jnp.concatenate([grad_own.astype(bf16), grad_other])
            grad_own = lax.psum_scatter(grads, "path", scatter_dimension=0, tiled=True).astype(f32)
            grad_other = jnp.zeros(grad_own.shape, bf16)
            small = lax.psum(small, "path")
            small_other = jnp.zeros_like(small)
        own_rows = w_mid_copy.shape[1]
        block = min(64, own_rows)
        mid_block = pl.BlockSpec((block, hidden), lambda i: (i, 0))
        whole = lambda *shape: pl.BlockSpec(shape, lambda i: (0,) * len(shape))
        in_block, vec_block = whole(count, hidden), whole(3, 1, hidden)
        outs = pl.pallas_call(
            lambda *refs: update(paths * cores, *refs),
            grid=(own_rows // block,),
            in_specs=[
                mid_block, mid_block, whole(SMALL_ROWS, hidden), whole(SMALL_ROWS, hidden),
                mid_block, mid_block, in_block, in_block, vec_block, vec_block,
            ],
            out_specs=[
                pl.BlockSpec(memory_space=pltpu.SMEM),
                in_block, mid_block, vec_block, in_block, mid_block, vec_block, in_block, mid_block,
            ],
            out_shape=[
                jax.ShapeDtypeStruct((1,), f32),
                jax.ShapeDtypeStruct((count, hidden), f32),
                jax.ShapeDtypeStruct((own_rows, hidden), f32),
                jax.ShapeDtypeStruct((3, 1, hidden), f32),
                jax.ShapeDtypeStruct((count, hidden), f32),
                jax.ShapeDtypeStruct((own_rows, hidden), f32),
                jax.ShapeDtypeStruct((3, 1, hidden), f32),
                jax.ShapeDtypeStruct((count, hidden), bf16),
                jax.ShapeDtypeStruct((own_rows, hidden), bf16),
            ],
            compiler_params=pltpu.CompilerParams(vmem_limit_bytes=VMEM_LIMIT),
            cost_estimate=pl.CostEstimate(flops=0, bytes_accessed=10 << 20, transcendentals=0),
            name="update",
        )(
            grad_own, grad_other, small, small_other, mom_mid[0], w_mid_master[0],
            mom_in[0], w_in_master[0], mom_vec.transpose(1, 0, 2), vectors,
        )
        value, new_w_in, new_w_mid, new_vec, new_mom_in, new_mom_mid, new_mom_vec, in_copy, mid_copy = outs
        return (
            value,
            new_w_in[None],
            new_w_mid[None],
            new_vec.transpose(1, 0, 2),
            new_mom_in[None],
            new_mom_mid[None],
            new_mom_vec.transpose(1, 0, 2),
            in_copy[None],
            mid_copy[None],
        )

    return shards


def solution(mesh):
    vectors = P("vol", None, None)
    middle = P("vol", "path", None)
    in_specs = (
        P(None, "path"),
        P(None, "path"),
        P("vol", "path"),
        P(None, "vol", "path"),
        P(),
        vectors,
        middle,
        vectors,
        vectors,
        middle,
        vectors,
        middle,
        vectors,
    )
    out_specs = (P("vol"), vectors, middle, vectors, vectors, middle, vectors, vectors, middle)
    return jax.shard_map(step_of(mesh), mesh=mesh, in_specs=in_specs, out_specs=out_specs, check_vma=False)
```

time: 100 us -> 36.2 us (0.36)
  matrix products: 25.9 us -> 0 us
  between operations: 25.7 us -> 0.79 us
  Pallas kernels: 0 us -> 19.3 us
  other arithmetic: 14.2 us -> 1.44 us
  waiting for transfers between devices: 11.6 us -> 3.79 us
  starting transfers between devices: 15.9 us -> 8.31 us
  blocking collectives: 3.87 us -> 0 us
    dot_general x5 -> x0, matrix products: 25.9 us -> none  [the longest x1 8.62 us: row_product(): lax.dot_general(hidden_one, d_two_low, (((0,), (0,)), ((), ())), preferre...]
    pallas_call x0 -> x4, Pallas kernels: none -> 19.3 us  [the longest x1 7.19 us: shards(): call(lambda *refs: backward(flip_of, *refs), (jax.ShapeDtypeStruct((width...]
    reduce_scatter x1 -> x0, waiting for transfers between devices: 10.9 us -> none  [shards(): lax.psum_scatter(row_product(hidden_one, d_two_low).astype(jnp.bfloat16),...]
    ppermute x4 -> x7, starting transfers between devices: 15.8 us -> 8.31 us  [the longest x4 7.2 us: shards(): lax.ppermute(rows, 'vol', [(here, (here + below) % levels) for here in ra...]
    convert_element_type x2 -> x1, other arithmetic: 6.62 us -> 0.73 us  [shards(): decisions[date - 1].astype(f32)]
    reduce_sum x3 -> x0, other arithmetic: 5.44 us -> none  [the longest x1 4.22 us: network_pass(): d_bias_two = jnp.sum(d_pre_two, axis=0)]
    psum x1 -> x0, blocking collectives: 3.87 us -> none  [shards(): lax.psum((d_first, d_vectors, value_local), 'path')]
    ppermute x4 -> x7, waiting for transfers between devices: 0.01 us -> 3.79 us  [the longest x4 2.84 us: shards(): lax.ppermute(rows, 'vol', [(here, (here + below) % levels) for here in ra...]
  transfers between devices with their start and end apart: 7 -> 7, of which waited for: 1 -> 3; matrix products, arithmetic and copies ran while one was open for 31% -> 4% of each run, Pallas kernels for 0% -> 25%
where the time goes in v1:
time: 36.2 us; the launch traced here: 35.9 us
  Pallas kernels  19.3 us (53%)
  starting transfers between devices  8.31 us (23%)
  waiting for transfers between devices  3.79 us (10%)
  local copies, waits for them, and re-layouts  2.27 us (6%)
  other arithmetic  1.44 us (4%)
  between operations  0.79 us (2%)
    ppermute x4, starting transfers between devices, shards(): lax.ppermute(rows, 'vol', [(here, (here + below) % levels) for here in ra...  7.2 us
    pallas_call x1, Pallas kernels, shards(): call(lambda *refs: backward(flip_of, *refs), (jax.ShapeDtypeStruct((width...  7.19 us
    pallas_call x1, Pallas kernels, shards(): call(second_layer, (jax.ShapeDtypeStruct((paths, hidden), bf16), jax.Shap...  6.47 us
    pallas_call x1, Pallas kernels, shards(): pl.pallas_call(lambda *refs: update(paths * cores, *refs), grid=(own_rows...  3.95 us
    ppermute x4, waiting for transfers between devices, shards(): lax.ppermute(rows, 'vol', [(here, (here + below) % levels) for here in ra...  2.84 us
    unnamed x26, local copies, waits for them, and re-layouts  2.27 us
    pallas_call x1, Pallas kernels, shards(): call(lambda *refs: first_layer(flip_of, *refs), (jax.ShapeDtypeStruct((pa...  1.64 us
    ppermute x3, starting transfers between devices, swap(): return lax.ppermute(value, 'path', [(0, 1), (1, 0)])  1.11 us
  transfers between devices with their start and end apart: 7, of which 3 were waited for; matrix products, arithmetic and copies ran while one was open for 4% of the time, Pallas kernels for 25%

profile of v1, /device:TPU:0, one launch (start us, length us, event | category | flops | bytes accessed | tf_op | source)
XLA Modules:
  0.0 35.9 jit_solution(14642071641984935713)
XLA Ops:
  0.6 0.5 %collective-permute-start = (bf16[512,1024]{1,0:T(8,128)(2,1)}, bf16[512,1024]{1,0:T(8,128)(2,1)S(1)}, u32[]{:S(2)}, u32[]{:S(2)}) collective-permute-start(bf16[512,1024]{1,0:T(8,128)(2,1)} %bitcast.31), channel_id=1, source_target_pairs={{0,1},{1,0},{2,3},{3,2},{4,5},{5,4},{6,7},{7,6},{8,9},{9,8},{10,11... | collective-permute-start | bytes 3145736 | tf_op jit(solution)/shard_map/ppermute | solution.py:218
  1.2 0.7 %convert_bitcast_fusion.2 = (f32[1,1024]{1,0:T(1,128)S(1)}, f32[1,1024]{1,0:T(1,128)S(1)}, f32[1,1024]{1,0:T(1,128)S(1)}) fusion(s32[3,1,1024]{2,1,0:T(1,128)} %param.16), kind=kLoop, calls=%fused_computation.3 | loop fusion | flops 3072 | bytes 24576 | tf_op jit(solution)/shard_map/convert_element_type | solution.py:237
  1.9 0.7 %pad_maximum_fusion.own = f32[4,1024]{1,0:T(4,128)S(1)} fusion(f32[1,1024]{1,0:T(1,128)S(1)} %get-tuple-element.42, f32[1,1024]{1,0:T(1,128)S(1)} %get-tuple-element.43, f32[1,1024]{1,0:T(1,128)S(1)} %get-tuple-element.41, f32[1,1024]{1,0:T(1,128)} %param.15), kind=kLoop, calls=%fused_computation | loop fusion | flops 12288 | bytes 32768 | tf_op jit(solution)/shard_map/concatenate | solution.py:236
  2.6 2.6 %collective-permute-start.4 = (f32[4,1024]{1,0:T(4,128)S(1)}, f32[4,1024]{1,0:T(4,128)S(1)}, u32[]{:S(2)}, u32[]{:S(2)}) collective-permute-start(f32[4,1024]{1,0:T(4,128)S(1)} %pad_maximum_fusion.own), channel_id=1, source_target_pairs={{0,8},{2,10},{4,12},{6,14},{8,16},{10,18},{12,20},{14,22},{16,24},... | collective-permute-start | bytes 49160 | tf_op jit(solution)/shard_map/ppermute | solution.py:240
  5.2 2.4 %collective-permute-start.3 = (f32[4,1024]{1,0:T(4,128)S(1)}, f32[4,1024]{1,0:T(4,128)S(1)}, u32[]{:S(2)}, u32[]{:S(2)}) collective-permute-start(f32[4,1024]{1,0:T(4,128)S(1)} %pad_maximum_fusion.own), channel_id=1, source_target_pairs={{0,6},{2,8},{4,10},{6,12},{8,14},{10,16},{12,18},{14,20},{16,22},{... | collective-permute-start | bytes 49160 | tf_op jit(solution)/shard_map/ppermute | solution.py:240
  7.7 1.5 %collective-permute-start.2 = (f32[4,1024]{1,0:T(4,128)S(1)}, f32[4,1024]{1,0:T(4,128)S(1)}, u32[]{:S(2)}, u32[]{:S(2)}) collective-permute-start(f32[4,1024]{1,0:T(4,128)S(1)} %pad_maximum_fusion.own), channel_id=1, source_target_pairs={{0,4},{2,6},{4,8},{6,10},{8,12},{10,14},{12,16},{14,18},{16,20},{1... | collective-permute-start | bytes 49160 | tf_op jit(solution)/shard_map/ppermute | solution.py:240
  9.2 0.6 %collective-permute-start.1 = (f32[4,1024]{1,0:T(4,128)S(1)}, f32[4,1024]{1,0:T(4,128)S(1)}, u32[]{:S(2)}, u32[]{:S(2)}) collective-permute-start(f32[4,1024]{1,0:T(4,128)S(1)} %pad_maximum_fusion.own), channel_id=1, source_target_pairs={{0,2},{2,4},{4,6},{6,8},{8,10},{10,12},{12,14},{14,16},{16,18},{18... | collective-permute-start | bytes 49160 | tf_op jit(solution)/shard_map/ppermute | solution.py:240
  9.8 0.7 %copy-done.4 = f32[1,3,1024]{2,0,1:T(1,128)S(1)} copy-done((f32[1,3,1024]{2,0,1:T(1,128)S(1)}, f32[1,3,1024]{2,0,1:T(1,128)}, u32[]{:S(2)}) %copy-start.4) | copy-done | bytes 12312
  10.5 0.8 %copy-done.8 = bf16[1,16,1024]{2,1,0:T(8,128)(2,1)S(1)} copy-done((bf16[1,16,1024]{2,1,0:T(8,128)(2,1)S(1)}, bf16[1,16,1024]{2,1,0:T(8,128)(2,1)}, u32[]{:S(2)}) %copy-start.8) | copy-done | bytes 32792
  11.3 0.8 %copy-done.9 = bf16[16,1024]{1,0:T(8,128)(2,1)S(1)} copy-done((bf16[16,1024]{1,0:T(8,128)(2,1)S(1)}, bf16[16,1024]{1,0:T(8,128)(2,1)}, u32[]{:S(2)}) %copy-start.9) | copy-done | bytes 32792
  12.0 1.6 %first_layer.1 = (bf16[1024,1024]{1,0:T(8,128)(2,1)S(1)}, bf16[1024,1024]{1,0:T(8,128)(2,1)S(1)}) custom-call(bf16[16,1024]{1,0:T(8,128)(2,1)S(1)} %copy-done.9, bf16[16,1024]{1,0:T(8,128)(2,1)S(1)} %bitcast.34, f32[3,1,1024]{2,1,0:T(1,128)S(1)} %bitcast.27), custom_call_target="tpu_custom_call" | custom-call | flops 2147483648 | bytes 1048576 | tf_op jit(solution)/shard_map/first_layer/pallas_call | solution.py:244
  13.7 0.0 collective-permute-done.4.low4
  13.7 0.0 collective-permute-done.3.low3
  13.7 0.4 %collective-permute-done.2.low2 = f32[4,1024]{1,0:T(4,128)S(1)} collective-permute-done((f32[4,1024]{1,0:T(4,128)S(1)}, f32[4,1024]{1,0:T(4,128)S(1)}, u32[]{:S(2)}, u32[]{:S(2)}) %collective-permute-start.2) | collective-permute-done | bytes 16416 | tf_op jit(solution)/shard_map/ppermute | solution.py:240
  14.1 2.4 %collective-permute-done.1.low1 = f32[4,1024]{1,0:T(4,128)S(1)} collective-permute-done((f32[4,1024]{1,0:T(4,128)S(1)}, f32[4,1024]{1,0:T(4,128)S(1)}, u32[]{:S(2)}, u32[]{:S(2)}) %collective-permute-start.1) | collective-permute-done | bytes 16416 | tf_op jit(solution)/shard_map/ppermute | solution.py:240
  16.5 0.0 collective-permute-done.w_other.refs_3_
  16.6 0.0 copy-done.11
  16.6 0.0 copy-done.12
  16.6 0.0 copy-start.10
  16.6 6.5 %second_layer.1 = (bf16[1024,1024]{1,0:T(8,128)(2,1)S(1)}, bf16[512,1024]{1,0:T(8,128)(2,1)S(1)}, f32[8,1024]{1,0:T(8,128)S(1)}) custom-call(bf16[1024,1024]{1,0:T(8,128)(2,1)S(1)} %get-tuple-element.25.hidden_one.refs_0_, bf16[512,1024]{1,0:T(8,128)(2,1)S(1)} %bitcast.32, bf16[512,1024]{1,0:T(8,128)(2,1)S(1)} %collective-permute-done.w_other.refs_3_, ...), custom_call_target="tpu_custom_call" | custom-call | flops 4294967296 | bytes 1048576 | tf_op jit(solution)/shard_map/second_layer/pallas_call | solution.py:252
  23.1 0.1 collective-permute-start.5
  23.1 0.0 copy-done.10
  23.2 0.0 copy-start
  23.2 0.0 copy-start.1
  23.2 0.0 copy-start.2
  23.2 0.0 copy-start.3
  23.2 0.0 copy-start.6
  23.2 7.2 %backward.1 = (f32[512,1024]{1,0:T(8,128)S(1)}, f32[24,1024]{1,0:T(8,128)S(1)}) custom-call(bf16[1024,1024]{1,0:T(8,128)(2,1)S(1)} %get-tuple-element.25.hidden_one.refs_0_, bf16[1024,1024]{1,0:T(8,128)(2,1)S(1)} %get-tuple-element.26.refs_1_, bf16[512,1024]{1,0:T(8,128)(2,1)S(1)} %bitcast.33, bf16[512,1024]{1,0:T(8,128)(2,1)S(1)} %collective-permute-done.w_other.refs_3_, ...), custom_call_target="tpu_custom_call" | custom-call | flops 4294967296 | bytes 1048576 | tf_op jit(solution)/shard_map/backward/pallas_call | solution.py:270
  30.4 0.5 %collective-permute-start.6 = (f32[24,1024]{1,0:T(8,128)S(1)}, f32[24,1024]{1,0:T(8,128)S(1)}, u32[]{:S(2)}, u32[]{:S(2)}) collective-permute-start(f32[24,1024]{1,0:T(8,128)S(1)} %get-tuple-element.31.refs_2_), channel_id=1, source_target_pairs={{0,1},{1,0},{2,3},{3,2},{4,5},{5,4},{6,7},{7,6},{8,9},{9,8},{10,11... | collective-permute-start | bytes 294920 | tf_op jit(solution)/shard_map/ppermute | solution.py:218
  30.9 0.9 %collective-permute-done.6.refs_3_ = f32[24,1024]{1,0:T(8,128)S(1)} collective-permute-done((f32[24,1024]{1,0:T(8,128)S(1)}, f32[24,1024]{1,0:T(8,128)S(1)}, u32[]{:S(2)}, u32[]{:S(2)}) %collective-permute-start.6) | collective-permute-done | bytes 98336 | tf_op jit(solution)/shard_map/ppermute | solution.py:218
  31.9 0.0 collective-permute-done.5.refs_1_
  31.9 4.0 %update.1 = (f32[1]{0:T(128)}, f32[16,1024]{1,0:T(8,128)}, f32[512,1024]{1,0:T(8,128)}, f32[3,1,1024]{2,1,0:T(1,128)}, f32[16,1024]{1,0:T(8,128)}, /*index=5*/f3...) custom-call(f32[512,1024]{1,0:T(8,128)S(1)} %get-tuple-element.29.refs_0_, ...), custom_call_target="tpu_custom_call" | custom-call | bytes 10485760 | tf_op jit(solution)/shard_map/update/pallas_call | solution.py:294
  (14 shorter events, 0.0 us)
Async XLA Ops:
  0.6 15.9 %collective-permute-start = (bf16[512,1024]{1,0:T(8,128)(2,1)}, bf16[512,1024]{1,0:T(8,128)(2,1)S(1)}, u32[]{:S(2)}, u32[]{:S(2)}) collective-permute-start(bf16[512,1024]{1,0:T(8,128)(2,1)} %bitcast.31), channel_id=1, source_target_pairs={{0,1},{1,0},{2,3},{3,2},{4,5},{5,4},{6,7},{7,6},{8,9},{9,8},{10,11... | collective-permute-start | bytes 3145736 | tf_op jit(solution)/shard_map/ppermute | solution.py:218
  2.6 11.1 %collective-permute-start.4 = (f32[4,1024]{1,0:T(4,128)S(1)}, f32[4,1024]{1,0:T(4,128)S(1)}, u32[]{:S(2)}, u32[]{:S(2)}) collective-permute-start(f32[4,1024]{1,0:T(4,128)S(1)} %pad_maximum_fusion.own), channel_id=1, source_target_pairs={{0,8},{2,10},{4,12},{6,14},{8,16},{10,18},{12,20},{14,22},{16,24},... | collective-permute-start | bytes 49160 | tf_op jit(solution)/shard_map/ppermute | solution.py:240
  5.2 8.5 %collective-permute-start.3 = (f32[4,1024]{1,0:T(4,128)S(1)}, f32[4,1024]{1,0:T(4,128)S(1)}, u32[]{:S(2)}, u32[]{:S(2)}) collective-permute-start(f32[4,1024]{1,0:T(4,128)S(1)} %pad_maximum_fusion.own), channel_id=1, source_target_pairs={{0,6},{2,8},{4,10},{6,12},{8,14},{10,16},{12,18},{14,20},{16,22},{... | collective-permute-start | bytes 49160 | tf_op jit(solution)/shard_map/ppermute | solution.py:240
  7.7 6.4 %collective-permute-start.2 = (f32[4,1024]{1,0:T(4,128)S(1)}, f32[4,1024]{1,0:T(4,128)S(1)}, u32[]{:S(2)}, u32[]{:S(2)}) collective-permute-start(f32[4,1024]{1,0:T(4,128)S(1)} %pad_maximum_fusion.own), channel_id=1, source_target_pairs={{0,4},{2,6},{4,8},{6,10},{8,12},{10,14},{12,16},{14,18},{16,20},{1... | collective-permute-start | bytes 49160 | tf_op jit(solution)/shard_map/ppermute | solution.py:240
  9.2 7.3 %collective-permute-start.1 = (f32[4,1024]{1,0:T(4,128)S(1)}, f32[4,1024]{1,0:T(4,128)S(1)}, u32[]{:S(2)}, u32[]{:S(2)}) collective-permute-start(f32[4,1024]{1,0:T(4,128)S(1)} %pad_maximum_fusion.own), channel_id=1, source_target_pairs={{0,2},{2,4},{4,6},{6,8},{8,10},{10,12},{12,14},{14,16},{16,18},{18... | collective-permute-start | bytes 49160 | tf_op jit(solution)/shard_map/ppermute | solution.py:240
  9.8 0.7 %copy-start.4 = (f32[1,3,1024]{2,0,1:T(1,128)S(1)}, f32[1,3,1024]{2,0,1:T(1,128)}, u32[]{:S(2)}) copy-start(f32[1,3,1024]{2,0,1:T(1,128)} %param.20) | copy-start | bytes 36868
  10.5 0.8 %copy-start.8 = (bf16[1,16,1024]{2,1,0:T(8,128)(2,1)S(1)}, bf16[1,16,1024]{2,1,0:T(8,128)(2,1)}, u32[]{:S(2)}) copy-start(bf16[1,16,1024]{2,1,0:T(8,128)(2,1)} %param.21) | copy-start | bytes 98308
  11.3 0.8 %copy-start.9 = (bf16[16,1024]{1,0:T(8,128)(2,1)S(1)}, bf16[16,1024]{1,0:T(8,128)(2,1)}, u32[]{:S(2)}) copy-start(bf16[16,1024]{1,0:T(8,128)(2,1)} %refs_5_.1) | copy-start | bytes 98308
  12.0 4.5 %copy-start.5 = (f32[1,3,1024]{2,0,1:T(1,128)S(1)}, f32[1,3,1024]{2,0,1:T(1,128)}, u32[]{:S(2)}) copy-start(f32[1,3,1024]{2,0,1:T(1,128)} %param.20) | copy-start | bytes 36868
  12.0 4.5 %copy-start.7 = (bf16[1,512,1024]{2,1,0:T(8,128)(2,1)S(1)}, bf16[1,512,1024]{2,1,0:T(8,128)(2,1)}, u32[]{:S(2)}) copy-start(bf16[1,512,1024]{2,1,0:T(8,128)(2,1)} %param.22) | copy-start | bytes 3145732
  12.0 4.5 %copy-start.11 = (f32[4,1024]{1,0:T(4,128)S(1)}, f32[4,1024]{1,0:T(4,128)}, u32[]{:S(2)}) copy-start(f32[4,1024]{1,0:T(4,128)} %payoff.1) | copy-start | bytes 49156
  12.0 4.5 %copy-start.12 = (s32[4,2]{0,1:T(2,128)S(1)}, s32[4,2]{0,1:T(2,128)}, u32[]{:S(2)}) copy-start(s32[4,2]{0,1:T(2,128)} %param.17) | copy-start | bytes 100
  16.6 6.6 %copy-start.10 = (bf16[16,1024]{1,0:T(8,128)(2,1)S(1)}, bf16[16,1024]{1,0:T(8,128)(2,1)}, u32[]{:S(2)}) copy-start(bf16[16,1024]{1,0:T(8,128)(2,1)} %refs_5_.1) | copy-start | bytes 98308
  23.1 8.8 %collective-permute-start.5 = (bf16[512,1024]{1,0:T(8,128)(2,1)S(1)}, bf16[512,1024]{1,0:T(8,128)(2,1)S(1)}, u32[]{:S(2)}, u32[]{:S(2)}) collective-permute-start(bf16[512,1024]{1,0:T(8,128)(2,1)S(1)} %get-tuple-element.30), channel_id=1, source_target_pairs={{0,1},{1,0},{2,3},{3,2},{4,5},{5,4},{6,7},{7,6},{8,9},{9,8},{10,11... | collective-permute-start | bytes 3145736 | tf_op jit(solution)/shard_map/ppermute | solution.py:218
  23.2 8.7 %copy-start = (f32[1,512,1024]{2,1,0:T(8,128)S(1)}, f32[1,512,1024]{2,1,0:T(8,128)}, u32[]{:S(2)}) copy-start(f32[1,512,1024]{2,1,0:T(8,128)} %param.24) | copy-start | bytes 6291460
  23.2 8.7 %copy-start.1 = (f32[1,512,1024]{2,1,0:T(8,128)S(1)}, f32[1,512,1024]{2,1,0:T(8,128)}, u32[]{:S(2)}) copy-start(f32[1,512,1024]{2,1,0:T(8,128)} %param.19) | copy-start | bytes 6291460
  23.2 8.7 %copy-start.2 = (f32[1,16,1024]{2,1,0:T(8,128)S(1)}, f32[1,16,1024]{2,1,0:T(8,128)}, u32[]{:S(2)}) copy-start(f32[1,16,1024]{2,1,0:T(8,128)} %param.23) | copy-start | bytes 196612
  23.2 8.7 %copy-start.3 = (f32[1,16,1024]{2,1,0:T(8,128)S(1)}, f32[1,16,1024]{2,1,0:T(8,128)}, u32[]{:S(2)}) copy-start(f32[1,16,1024]{2,1,0:T(8,128)} %param.18) | copy-start | bytes 196612
  23.2 8.7 %copy-start.6 = (f32[1,3,1024]{2,0,1:T(1,128)S(1)}, f32[1,3,1024]{2,0,1:T(1,128)}, u32[]{:S(2)}) copy-start(f32[1,3,1024]{2,0,1:T(1,128)} %param.25) | copy-start | bytes 36868
  30.4 1.5 %collective-permute-start.6 = (f32[24,1024]{1,0:T(8,128)S(1)}, f32[24,1024]{1,0:T(8,128)S(1)}, u32[]{:S(2)}, u32[]{:S(2)}) collective-permute-start(f32[24,1024]{1,0:T(8,128)S(1)} %get-tuple-element.31.refs_2_), channel_id=1, source_target_pairs={{0,1},{1,0},{2,3},{3,2},{4,5},{5,4},{6,7},{7,6},{8,9},{9,8},{10,11... | collective-permute-start | bytes 294920 | tf_op jit(solution)/shard_map/ppermute | solution.py:218

commit v2 on v1

v2 whole, which is shorter than its diff:
```python
import jax
import jax.numpy as jnp
from jax import lax
from jax.experimental import pallas as pl
from jax.experimental.pallas import tpu as pltpu
from jax.sharding import PartitionSpec as P

MOMENTUM = 0.9
STEP_SIZE = 0.01
LOWER_LEVELS = 4
SMALL_ROWS = 24
LANES = 128
VMEM_LIMIT = 30 * 1024 * 1024
F32, BF16 = jnp.float32, jnp.bfloat16
VMEM_SPEC = pl.BlockSpec(memory_space=pltpu.VMEM)
HBM_SPEC = pl.BlockSpec(memory_space=pltpu.HBM)


def far(value):
    return pltpu.with_memory_space_constraint(value, pltpu.HBM)


def shape(*dims, dtype=F32):
    return jax.ShapeDtypeStruct(dims, dtype)


def call(kernel, out_shape, in_specs, name, flops, out_specs=None, scratch=()):
    return pl.pallas_call(
        kernel,
        out_shape=out_shape,
        in_specs=in_specs,
        out_specs=out_specs or [VMEM_SPEC] * len(out_shape),
        scratch_shapes=list(scratch),
        compiler_params=pltpu.CompilerParams(vmem_limit_bytes=VMEM_LIMIT),
        cost_estimate=pl.CostEstimate(flops=flops, bytes_accessed=1 << 20, transcendentals=0),
        name=name,
    )


def half_columns(flip, half, width):
    return pl.ds(pl.multiple_of((flip ^ half) * width, width), width)


def is_active(flags):
    return flags[0, 0] > 0.5


def prepare(
    terminal, decisions, ranges, payoff, factors, w_in, vectors,
    rows, flags, payoff_out, factors_out, w_in_out, vectors_out,
    terminal_here, decisions_here, ranges_here, sems,
):
    copies = [
        pltpu.make_async_copy(source, target, sems.at[index])
        for index, (source, target) in enumerate(
            (
                (ranges, ranges_here),
                (terminal, terminal_here),
                (decisions, decisions_here),
                (payoff, payoff_out),
                (factors, factors_out),
                (w_in, w_in_out),
                (vectors, vectors_out),
            )
        )
    ]
    for copy in copies:
        copy.start()
    for copy in copies:
        copy.wait()
    level = lax.axis_index("vol")
    dates = payoff.shape[0]
    rows[0:1, :] = terminal_here[...]
    for date in range(dates - 1, 0, -1):
        low, high = ranges_here[0, date], ranges_here[1, date]
        inside = jnp.logical_and(level >= low, level <= high)
        chosen = decisions_here[date - 1].astype(F32)
        taken = jnp.where(level > high, 1.0, jnp.where(inside, chosen, 0.0))
        rows[dates - date : dates - date + 1, :] = taken
    low, high = ranges_here[0, 0], ranges_here[1, 0]
    active = jnp.logical_and(level >= low, level <= high)
    flags[0:8, :] = jnp.full((8, LANES), jnp.where(active, 1.0, 0.0))
    flags[8:16, :] = jnp.full((8, LANES), jnp.where(level > high, 1.0, 0.0))


def silu_parts(preact):
    half = 0.5 * preact
    bent = jnp.tanh(half)
    upper = 1.0 + bent
    act = half * upper
    return act, upper + act * (1.0 - bent)


def first_layer(flip_of, flags, factors, w_in, vectors, hidden_one, slope_one):
    @pl.when(is_active(flags))
    def _():
        flip = flip_of()
        hidden = w_in.shape[1]
        width, paths, tile, rows = hidden // 2, factors.shape[1], 256, 16
        for half in range(2):
            columns = half_columns(flip, half, width)
            weights = w_in[:, columns]
            bias = vectors[0, :, columns]
            place = slice(half * width, (half + 1) * width)
            for start in range(0, paths, tile):
                pre = lax.dot_general(
                    factors[:, start : start + tile],
                    weights,
                    (((0,), (0,)), ((), ())),
                    preferred_element_type=F32,
                )
                for row in range(0, tile, rows):
                    act, slope = silu_parts(pre[row : row + rows] + bias)
                    here = slice(start + row, start + row + rows)
                    hidden_one[here, place] = act.astype(BF16)
                    slope_one[here, place] = (0.5 * slope).astype(BF16)


def continuation(level, payoff, row_sets):
    dates = payoff.shape[0]
    conts = [jnp.where(level >= below, rows[0:1, :], 0.0) for below, rows in enumerate(row_sets)]
    for date in range(dates - 1, 0, -1):
        updated = []
        for below in range(len(conts) - 1):
            taken = row_sets[below][dates - date : dates - date + 1, :]
            value = taken * (payoff[date : date + 1, :] + conts[below + 1]) + (1.0 - taken) * conts[below]
            updated.append(jnp.where(level >= below, value, 0.0))
        conts = updated
    return conts


def second_layer(
    flags, hidden_one, w_own, w_other, vectors, payoff, own, low1, low2, low3, low4,
    d_two, grad_other, sums, gains, pre, weighted, act_two, parts,
):
    level = lax.axis_index("vol")
    paths, hidden = hidden_one.shape
    width, tile, rows, chunks = hidden // 2, 256, 16, 4
    lane_tiles = hidden // LANES
    row_sets = [ref[...] for ref in (own, low1, low2, low3, low4)]
    cont_here, cont_below = continuation(level, payoff, row_sets)
    gain = payoff[0:1, :] + cont_below - cont_here
    base_value = flags[8, 0] * jnp.sum(gain) + jnp.sum(cont_here)

    @pl.when(jnp.logical_not(is_active(flags)))
    def _():
        grad_other[...] = jnp.zeros(grad_other.shape, BF16)
        sums[...] = jnp.zeros(sums.shape, F32)
        sums[2:3, :] = jnp.full((1, hidden), base_value, F32)

    @pl.when(is_active(flags))
    def _():
        gains[...] = jnp.transpose(jnp.broadcast_to(gain, (LANES, paths)))
        bias, head = vectors[1], vectors[2]
        half_head = 0.5 * head
        ones = jnp.ones((2 * LANES, LANES), BF16)
        bias_sums = [jnp.zeros((8, LANES), F32) for _ in range(lane_tiles)]
        head_sums = [jnp.zeros((8, LANES), F32) for _ in range(lane_tiles)]
        value_sum = jnp.zeros((rows, LANES), F32)

        def product(start, columns):
            here = slice(start, start + tile)
            return jnp.dot(
                hidden_one[here, :width], w_own[:, columns], preferred_element_type=F32
            ) + jnp.dot(hidden_one[here, width:], w_other[:, columns], preferred_element_type=F32)

        count = paths // tile
        for step in range(count + 1):
            slot, last = step % 2, (step - 1) % 2
            for chunk in range(chunks):
                if step < count:
                    columns = slice(chunk * hidden // chunks, (chunk + 1) * hidden // chunks)
                    pre[slot, :, columns] = product(step * tile, columns)
                if step > 0:
                    for row in range(chunk * tile // chunks, (chunk + 1) * tile // chunks, rows):
                        here = slice(row, row + rows)
                        act, slope = silu_parts(pre[last, here, :] + bias)
                        weighted[last, here, :] = slope * half_head
                        act_two[last, here, :] = act
                        terms = act * head
                        part = terms[:, :LANES]
                        for lane in range(1, lane_tiles):
                            part += terms[:, lane * LANES : (lane + 1) * LANES]
                        upper = part.astype(BF16)
                        parts[last, here, :LANES] = upper
                        parts[last, here, LANES:] = (part - upper.astype(F32)).astype(BF16)
            if step > 0:
                start = (step - 1) * tile
                logits = jnp.dot(parts[last], ones, preferred_element_type=F32)
                for row in range(0, tile, rows):
                    here = slice(row, row + rows)
                    there = slice(start + row, start + row + rows)
                    chance = 0.5 + 0.5 * jnp.tanh(0.5 * logits[here])
                    weight = gains[there, :] * chance
                    value_sum += weight
                    d_logit = weight * (chance - 1.0)
                    for lane in range(lane_tiles):
                        place = slice(lane * LANES, (lane + 1) * LANES)
                        d_pre = d_logit * weighted[last, here, place]
                        scaled = d_logit * act_two[last, here, place]
                        d_two[there, place] = d_pre.astype(BF16)
                        for part in range(0, rows, 8):
                            bias_sums[lane] += d_pre[part : part + 8]
                            head_sums[lane] += scaled[part : part + 8]
        grad_other[...] = lax.dot_general(
            hidden_one[:, width:], d_two[...], (((0,), (0,)), ((), ())), preferred_element_type=F32
        ).astype(BF16)
        value_total = base_value + jnp.sum(value_sum) / LANES
        for lane in range(lane_tiles):
            place = slice(lane * LANES, (lane + 1) * LANES)
            sums[0:1, place] = jnp.sum(bias_sums[lane], axis=0, keepdims=True)
            sums[1:2, place] = jnp.sum(head_sums[lane], axis=0, keepdims=True)
        sums[2:3, :] = jnp.full((1, hidden), value_total, F32)
        sums[3:8, :] = jnp.zeros((5, hidden), F32)


def first_gradients(flip_of, flags, d_two, w_own, w_other, slope_one, factors, sums, small, d_one):
    count = factors.shape[0]
    hidden = d_two.shape[1]
    small[0 : count + 1, :] = jnp.zeros((count + 1, hidden), F32)
    small[count + 1 : count + 4, :] = sums[0:3, :]
    small[count + 4 : SMALL_ROWS, :] = jnp.zeros((SMALL_ROWS - count - 4, hidden), F32)

    @pl.when(is_active(flags))
    def _():
        flip = flip_of()
        paths = d_two.shape[0]
        width, tile, rows = hidden // 2, 256, 16
        for half, weights in enumerate((w_own, w_other)):
            place = slice(half * width, (half + 1) * width)
            bias_sum = jnp.zeros((8, width), F32)
            for start in range(0, paths, tile):
                d_hidden = lax.dot_general(
                    d_two[start : start + tile, :],
                    weights[...],
                    (((1,), (1,)), ((), ())),
                    preferred_element_type=F32,
                )
                for row in range(0, tile, rows):
                    here = slice(start + row, start + row + rows)
                    d_pre = d_hidden[row : row + rows] * slope_one[here, place].astype(F32)
                    d_one[here, place] = d_pre.astype(BF16)
                    for part in range(0, rows, 8):
                        bias_sum += d_pre[part : part + 8]
            columns = half_columns(flip, half, width)
            small[0:count, columns] = jnp.dot(factors[...], d_one[:, place], preferred_element_type=F32)
            small[count : count + 1, columns] = jnp.sum(bias_sum, axis=0, keepdims=True)


def own_gradient(hidden_one, d_two):
    width = hidden_one.shape[1] // 2
    return lax.dot_general(
        hidden_one[:, :width], d_two[...], (((0,), (0,)), ((), ())), preferred_element_type=F32
    )


def plain_gradient(flags, hidden_one, d_two, grad_own):
    grad_own[...] = jnp.zeros(grad_own.shape, BF16)

    @pl.when(is_active(flags))
    def _():
        grad_own[...] = own_gradient(hidden_one, d_two).astype(BF16)


def half_update(flags, hidden_one, d_two, mom_mid, w_mid, mom_part, w_part):
    def store(momentum):
        mom_part[...] = momentum
        w_part[...] = w_mid[...] - STEP_SIZE * momentum

    @pl.when(is_active(flags))
    def _():
        store(MOMENTUM * mom_mid[...] + own_gradient(hidden_one, d_two))

    @pl.when(jnp.logical_not(is_active(flags)))
    def _():
        store(MOMENTUM * mom_mid[...])


def update(
    paths_total, block, mom_part, w_part, grad_other, small_own, small_other, mom_in, w_in, mom_vec, vec,
    value, new_w_in, new_w_mid, new_vec, new_mom_in, new_mom_mid, new_mom_vec, new_in_copy, new_mid_copy,
    w_in_here, w_mid_here, vec_here, mom_in_here, mom_mid_here, mom_vec_here, in_copy_here, mid_copy_here, sems,
):
    copies = []

    def send(source, target):
        copy = pltpu.make_async_copy(source, target, sems.at[len(copies)])
        copy.start()
        copies.append(copy)

    for start in range(0, mom_part.shape[0], block):
        here = pl.ds(start, block)
        received = grad_other[here, :].astype(F32)
        mom_mid_here[here, :] = mom_part[here, :] + received
        master = w_part[here, :] - STEP_SIZE * received
        w_mid_here[here, :] = master
        mid_copy_here[here, :] = master.astype(BF16)
        send(mom_mid_here.at[here], new_mom_mid.at[here])
        send(w_mid_here.at[here], new_w_mid.at[here])
        send(mid_copy_here.at[here], new_mid_copy.at[here])
    small = small_own[...] + small_other[...]
    count = mom_in.shape[0]
    mom_first = MOMENTUM * mom_in[...] + small[:count]
    first = w_in[...] - STEP_SIZE * mom_first
    mom_in_here[...] = mom_first
    w_in_here[...] = first
    in_copy_here[...] = first.astype(BF16)
    for row in range(3):
        mom_row = MOMENTUM * mom_vec[row] + small[count + row : count + row + 1]
        mom_vec_here[row] = mom_row
        vec_here[row] = vec[row] - STEP_SIZE * mom_row
    send(mom_in_here, new_mom_in)
    send(w_in_here, new_w_in)
    send(in_copy_here, new_in_copy)
    send(mom_vec_here, new_mom_vec)
    send(vec_here, new_vec)
    value[0] = small[count + 3, 0] / paths_total
    for copy in copies:
        copy.wait()


def step_of(mesh):
    levels, cores = mesh.shape["vol"], mesh.shape["path"]
    paired = cores == 2

    def flip_of():
        return lax.axis_index("path") if paired else 0

    def swap(value):
        return lax.ppermute(value, "path", [(0, 1), (1, 0)])

    def shards(
        factors, payoff, terminal, decisions, level_range, w_in_master, w_mid_master, vec_master,
        w_in_copy, w_mid_copy, mom_in, mom_mid, mom_vec,
    ):
        dates, paths = payoff.shape
        count, hidden = w_in_copy.shape[1:]
        width = hidden // 2
        square = 2 * paths * hidden * hidden
        if paired:
            w_own = w_mid_copy[0]
            w_other = swap(w_own)
        else:
            w_full = lax.all_gather(w_mid_copy[0], "path", axis=0, tiled=True)
            w_own, w_other = w_full[:width], w_full[width:]
        vec_hbm = vec_master.transpose(1, 0, 2)
        rows, flags, payoff_near, factors_near, w_in_near, vectors = call(
            prepare,
            (
                shape(dates, paths),
                shape(16, LANES),
                shape(dates, paths),
                shape(count, paths, dtype=BF16),
                shape(count, hidden, dtype=BF16),
                shape(3, 1, hidden),
            ),
            [HBM_SPEC] * 7,
            "prepare",
            0,
            scratch=(
                pltpu.VMEM((1, paths), F32),
                pltpu.VMEM((dates - 1, 1, paths), jnp.int32),
                pltpu.SMEM((2, dates), jnp.int32),
                pltpu.SemaphoreType.DMA((7,)),
            ),
        )(*(far(value) for value in (terminal, decisions, level_range.T, payoff, factors, w_in_copy[0], vec_hbm)))
        lower = [
            lax.ppermute(rows, "vol", [(here, (here + below) % levels) for here in range(levels)])
            for below in range(1, LOWER_LEVELS + 1)
        ]
        hidden_one, slope_one = call(
            lambda *refs: first_layer(flip_of, *refs),
            (shape(paths, hidden, dtype=BF16),) * 2,
            [VMEM_SPEC] * 4,
            "first_layer",
            square,
        )(flags, factors_near, w_in_near, vectors)
        d_two, grad_other, sums = call(
            second_layer,
            (
                shape(paths, hidden, dtype=BF16),
                shape(width, hidden, dtype=BF16),
                shape(8, hidden),
            ),
            [VMEM_SPEC] * 11,
            "second_layer",
            2 * square,
            scratch=(
                pltpu.VMEM((paths, LANES), F32),
                pltpu.VMEM((2, 256, hidden), F32),
                pltpu.VMEM((2, 256, hidden), F32),
                pltpu.VMEM((2, 256, hidden), F32),
                pltpu.VMEM((2, 256, 2 * LANES), BF16),
            ),
        )(flags, hidden_one, w_own, w_other, vectors, payoff_near, rows, *lower)
        if paired:
            grad_other = swap(grad_other)
        (small,) = call(
            lambda *refs: first_gradients(flip_of, *refs),
            (shape(SMALL_ROWS, hidden),),
            [VMEM_SPEC] * 7,
            "first_gradients",
            square,
            scratch=(pltpu.VMEM((paths, hidden), BF16),),
        )(flags, d_two, w_own, w_other, slope_one, factors_near, sums)
        if paired:
            small_other = swap(small)
            mom_part, w_part = call(
                half_update,
                (shape(width, hidden),) * 2,
                [VMEM_SPEC] * 5,
                "half_update",
                square,
            )(flags, hidden_one, d_two, mom_mid[0], w_mid_master[0])
        else:
            (grad_own,) = call(
                plain_gradient,
                (shape(width, hidden, dtype=BF16),),
                [VMEM_SPEC] * 3,
                "plain_gradient",
                square,
            )(flags, hidden_one, d_two)
            grads = jnp.concatenate([grad_own, grad_other])
            grads = lax.psum_scatter(grads, "path", scatter_dimension=0, tiled=True).astype(F32)
            mom_part = MOMENTUM * mom_mid[0] + grads
            w_part = w_mid_master[0] - STEP_SIZE * mom_part
            grad_other = jnp.zeros(grads.shape, BF16)
            small = lax.psum(small, "path")
            small_other = jnp.zeros_like(small)
        own_rows = w_mid_copy.shape[1]
        block = min(128, own_rows)
        outs = (
            shape(1),
            shape(count, hidden),
            shape(own_rows, hidden),
            shape(3, 1, hidden),
            shape(count, hidden),
            shape(own_rows, hidden),
            shape(3, 1, hidden),
            shape(count, hidden, dtype=BF16),
            shape(own_rows, hidden, dtype=BF16),
        )
        value, new_w_in, new_w_mid, new_vec, new_mom_in, new_mom_mid, new_mom_vec, in_copy, mid_copy = call(
            lambda *refs: update(paths * cores, block, *refs),
            outs,
            [VMEM_SPEC] * 9,
            "update",
            0,
            out_specs=[pl.BlockSpec(memory_space=pltpu.SMEM)] + [HBM_SPEC] * 8,
            scratch=[pltpu.VMEM(out.shape, out.dtype) for out in outs[1:]]
            + [pltpu.SemaphoreType.DMA((3 * (own_rows // block) + 5,))],
        )(
            mom_part, w_part, grad_other, small, small_other,
            mom_in[0], w_in_master[0], mom_vec.transpose(1, 0, 2), vectors,
        )
        return (
            value,
            new_w_in[None],
            new_w_mid[None],
            new_vec.transpose(1, 0, 2),
            new_mom_in[None],
            new_mom_mid[None],
            new_mom_vec.transpose(1, 0, 2),
            in_copy[None],
            mid_copy[None],
        )

    return shards


def solution(mesh):
    vectors = P("vol", None, None)
    middle = P("vol", "path", None)
    in_specs = (
        P(None, "path"),
        P(None, "path"),
        P("vol", "path"),
        P(None, "vol", "path"),
        P(),
        vectors,
        middle,
        vectors,
        vectors,
        middle,
        vectors,
        middle,
        vectors,
    )
    out_specs = (P("vol"), vectors, middle, vectors, vectors, middle, vectors, vectors, middle)
    return jax.shard_map(step_of(mesh), mesh=mesh, in_specs=in_specs, out_specs=out_specs, check_vma=False)
```

time: 36.2 us -> 26.3 us (0.73)
  the two profiles are of different devices: /device:TPU:0 before, /device:TPU:13 now
where the time goes in v2:
time: 26.3 us; the launch traced here: 26 us
  Pallas kernels  15.9 us (60%)
  starting transfers between devices  7.61 us (29%)
  waiting for transfers between devices  1.73 us (7%)
  between operations  0.76 us (3%)
    pallas_call x1, Pallas kernels, shards(): call(second_layer, (shape(paths, hidden, dtype=BF16), shape(width, hidden...  5.83 us
    ppermute x4, starting transfers between devices, shards(): lax.ppermute(rows, 'vol', [(here, (here + below) % levels) for here in ra...  4.76 us
    pallas_call x1, Pallas kernels, shards(): call(lambda *refs: update(paths * cores, block, *refs), outs, [VMEM_SPEC]...  3.1 us
    ppermute x3, starting transfers between devices, swap(): return lax.ppermute(value, 'path', [(0, 1), (1, 0)])  2.85 us
    pallas_call x1, Pallas kernels, shards(): call(lambda *refs: first_gradients(flip_of, *refs), (shape(SMALL_ROWS, hi...  2.83 us
    pallas_call x1, Pallas kernels, shards(): call(lambda *refs: first_layer(flip_of, *refs), (shape(paths, hidden, dty...  1.73 us
    ppermute x4, waiting for transfers between devices, shards(): lax.ppermute(rows, 'vol', [(here, (here + below) % levels) for here in ra...  1.73 us
    pallas_call x1, Pallas kernels, shards(): call(half_update, (shape(width, hidden),) * 2, [VMEM_SPEC] * 5, 'half_upd...  1.54 us
  transfers between devices with their start and end apart: 7, of which 1 were waited for; matrix products, arithmetic and copies ran while one was open for 0% of the time, Pallas kernels for 27%

profile of v2, /device:TPU:13, one launch (start us, length us, event | category | flops | bytes accessed | tf_op | source)
XLA Modules:
  0.0 26.0 jit_solution(817187293731570135)
XLA Ops:
  0.6 0.7 %collective-permute-start = (bf16[512,1024]{1,0:T(8,128)(2,1)}, bf16[512,1024]{1,0:T(8,128)(2,1)S(1)}, u32[]{:S(2)}, u32[]{:S(2)}) collective-permute-start(bf16[512,1024]{1,0:T(8,128)(2,1)} %bitcast.22), channel_id=1, source_target_pairs={{0,1},{1,0},{2,3},{3,2},{4,5},{5,4},{6,7},{7,6},{8,9},{9,8},{10,11... | collective-permute-start | bytes 3145736 | tf_op jit(solution)/shard_map/ppermute | solution.py:330
  1.4 0.9 %prepare.1 = (f32[4,1024]{1,0:T(4,128)S(1)}, f32[16,128]{1,0:T(8,128)S(1)}, f32[4,1024]{1,0:T(4,128)S(1)}, bf16[16,1024]{1,0:T(8,128)(2,1)S(1)}, bf16[16,1024]{1...) custom-call(f32[1,1024]{1,0:T(1,128)} %terminal.1, s32[3,1,1024]{2,1,0:T(1,128)} %decisions.1, s32[2,4]{1,0:T(2,128)} %bitcast.27, ...), custom_call_target="tpu_custom_call" | custom-call | bytes 1048576 | tf_op jit(solution)/shard_map/prepare/pallas_call | solution.py:347
  2.3 1.3 %collective-permute-start.4 = (f32[4,1024]{1,0:T(4,128)S(1)}, f32[4,1024]{1,0:T(4,128)S(1)}, u32[]{:S(2)}, u32[]{:S(2)}) collective-permute-start(f32[4,1024]{1,0:T(4,128)S(1)} %get-tuple-element.37.own), channel_id=1, source_target_pairs={{0,8},{2,10},{4,12},{6,14},{8,16},{10,18},{12,20},{14,22},{16,24},... | collective-permute-start | bytes 49160 | tf_op jit(solution)/shard_map/ppermute | solution.py:368
  3.6 2.2 %collective-permute-start.3 = (f32[4,1024]{1,0:T(4,128)S(1)}, f32[4,1024]{1,0:T(4,128)S(1)}, u32[]{:S(2)}, u32[]{:S(2)}) collective-permute-start(f32[4,1024]{1,0:T(4,128)S(1)} %get-tuple-element.37.own), channel_id=1, source_target_pairs={{0,6},{2,8},{4,10},{6,12},{8,14},{10,16},{12,18},{14,20},{16,22},{... | collective-permute-start | bytes 49160 | tf_op jit(solution)/shard_map/ppermute | solution.py:368
  5.8 1.2 %collective-permute-start.2 = (f32[4,1024]{1,0:T(4,128)S(1)}, f32[4,1024]{1,0:T(4,128)S(1)}, u32[]{:S(2)}, u32[]{:S(2)}) collective-permute-start(f32[4,1024]{1,0:T(4,128)S(1)} %get-tuple-element.37.own), channel_id=1, source_target_pairs={{0,4},{2,6},{4,8},{6,10},{8,12},{10,14},{12,16},{14,18},{16,20},{1... | collective-permute-start | bytes 49160 | tf_op jit(solution)/shard_map/ppermute | solution.py:368
  7.0 0.0 collective-permute-start.1
  7.0 0.0 copy-start.5
  7.0 1.7 %first_layer.1 = (bf16[1024,1024]{1,0:T(8,128)(2,1)S(1)}, bf16[1024,1024]{1,0:T(8,128)(2,1)S(1)}) custom-call(f32[16,128]{1,0:T(8,128)S(1)} %get-tuple-element.31.refs_0_.flags, bf16[16,1024]{1,0:T(8,128)(2,1)S(1)} %get-tuple-element.32.refs_1_.refs_5_, bf16[16,1024]{1,0:T(8,128)(2,1)S(1)} %get-tuple-element.33.refs_2_, ...), custom_call_target="tpu_custom_call" | custom-call | flops 2147483648 | bytes 1048576 | tf_op jit(solution)/shard_map/first_layer/pallas_call | solution.py:371
  8.8 0.0 collective-permute-done.4.low4
  8.8 0.0 collective-permute-done.3.low3
  8.8 0.0 collective-permute-done.2.low2
  8.8 1.7 %collective-permute-done.1.low1 = f32[4,1024]{1,0:T(4,128)S(1)} collective-permute-done((f32[4,1024]{1,0:T(4,128)S(1)}, f32[4,1024]{1,0:T(4,128)S(1)}, u32[]{:S(2)}, u32[]{:S(2)}) %collective-permute-start.1) | collective-permute-done | bytes 16416 | tf_op jit(solution)/shard_map/ppermute | solution.py:368
  10.5 0.0 collective-permute-done.w_other.refs_3_
  10.5 0.0 copy-done.5
  10.5 5.8 %second_layer.1 = (bf16[1024,1024]{1,0:T(8,128)(2,1)S(1)}, bf16[512,1024]{1,0:T(8,128)(2,1)S(1)}, f32[8,1024]{1,0:T(8,128)S(1)}) custom-call(f32[16,128]{1,0:T(8,128)S(1)} %get-tuple-element.31.refs_0_.flags, bf16[1024,1024]{1,0:T(8,128)(2,1)S(1)} %get-tuple-element.35.hidden_one, bf16[512,1024]{1,0:T(8,128)(2,1)S(1)} %bitcast.23, ...), custom_call_target="tpu_custom_call" | custom-call | flops 4294967296 | bytes 1048576 | tf_op jit(solution)/shard_map/second_layer/pallas_call | solution.py:378
  16.4 2.1 %collective-permute-start.5 = (bf16[512,1024]{1,0:T(8,128)(2,1)S(1)}, bf16[512,1024]{1,0:T(8,128)(2,1)S(1)}, u32[]{:S(2)}, u32[]{:S(2)}) collective-permute-start(bf16[512,1024]{1,0:T(8,128)(2,1)S(1)} %get-tuple-element.41), channel_id=1, source_target_pairs={{0,1},{1,0},{2,3},{3,2},{4,5},{5,4},{6,7},{7,6},{8,9},{9,8},{10,11... | collective-permute-start | bytes 3145736 | tf_op jit(solution)/shard_map/ppermute | solution.py:330
  18.4 0.0 copy-start
  18.4 0.0 copy-start.1
  18.4 2.8 %first_gradients.1.refs_3_ = f32[24,1024]{1,0:T(8,128)S(1)} custom-call(f32[16,128]{1,0:T(8,128)S(1)} %get-tuple-element.31.refs_0_.flags, bf16[1024,1024]{1,0:T(8,128)(2,1)S(1)} %get-tuple-element.38.d_two.refs_1_, bf16[512,1024]{1,0:T(8,128)(2,1)S(1)} %bitcast.24, bf16[512,1024]{1,0:T(8,128)(2,1)S(1)} %collective-permute-done.w_other.refs_3_, ...), custom_call_target="tpu_custom_call" | custom-call | flops 2147483648 | bytes 1048576 | tf_op jit(solution)/shard_map/first_gradients/pallas_call | solution.py:398
  21.3 0.0 collective-permute-start.6
  21.3 0.0 copy-done
  21.3 0.0 copy-done.1
  21.3 0.0 copy-start.2
  21.3 0.0 copy-start.3
  21.3 0.0 copy-start.4
  21.3 1.5 %half_update.1 = (f32[512,1024]{1,0:T(8,128)S(1)}, f32[512,1024]{1,0:T(8,128)S(1)}) custom-call(f32[16,128]{1,0:T(8,128)S(1)} %get-tuple-element.31.refs_0_.flags, bf16[1024,1024]{1,0:T(8,128)(2,1)S(1)} %get-tuple-element.35.hidden_one, bf16[1024,1024]{1,0:T(8,128)(2,1)S(1)} %get-tuple-element.38.d_two.refs_1_, f32[512,1024]{1,0:T(8,128)S(1)} %bitcast.17, ...), custom_call_target="tpu_custom_call" | custom-call | flops 2147483648 | bytes 1048576 | tf_op jit(solution)/shard_map/half_update/pallas_call | solution.py:408
  22.9 0.0 collective-permute-done.6.refs_4_
  22.9 0.0 collective-permute-done.5.refs_2_
  22.9 0.0 copy-done.2
  22.9 0.0 copy-done.3
  22.9 0.0 copy-done.4
  22.9 3.1 %update.1 = (f32[1]{0:T(128)}, f32[16,1024]{1,0:T(8,128)}, f32[512,1024]{1,0:T(8,128)}, f32[3,1,1024]{2,1,0:T(1,128)}, f32[16,1024]{1,0:T(8,128)}, /*index=5*/f3...) custom-call(f32[512,1024]{1,0:T(8,128)S(1)} %get-tuple-element.39.refs_0_, ...), custom_call_target="tpu_custom_call" | custom-call | bytes 1048576 | tf_op jit(solution)/shard_map/update/pallas_call | solution.py:443
Async XLA Ops:
  0.6 9.9 %collective-permute-start = (bf16[512,1024]{1,0:T(8,128)(2,1)}, bf16[512,1024]{1,0:T(8,128)(2,1)S(1)}, u32[]{:S(2)}, u32[]{:S(2)}) collective-permute-start(bf16[512,1024]{1,0:T(8,128)(2,1)} %bitcast.22), channel_id=1, source_target_pairs={{0,1},{1,0},{2,3},{3,2},{4,5},{5,4},{6,7},{7,6},{8,9},{9,8},{10,11... | collective-permute-start | bytes 3145736 | tf_op jit(solution)/shard_map/ppermute | solution.py:330
  2.3 6.5 %collective-permute-start.4 = (f32[4,1024]{1,0:T(4,128)S(1)}, f32[4,1024]{1,0:T(4,128)S(1)}, u32[]{:S(2)}, u32[]{:S(2)}) collective-permute-start(f32[4,1024]{1,0:T(4,128)S(1)} %get-tuple-element.37.own), channel_id=1, source_target_pairs={{0,8},{2,10},{4,12},{6,14},{8,16},{10,18},{12,20},{14,22},{16,24},... | collective-permute-start | bytes 49160 | tf_op jit(solution)/shard_map/ppermute | solution.py:368
  3.6 5.2 %collective-permute-start.3 = (f32[4,1024]{1,0:T(4,128)S(1)}, f32[4,1024]{1,0:T(4,128)S(1)}, u32[]{:S(2)}, u32[]{:S(2)}) collective-permute-start(f32[4,1024]{1,0:T(4,128)S(1)} %get-tuple-element.37.own), channel_id=1, source_target_pairs={{0,6},{2,8},{4,10},{6,12},{8,14},{10,16},{12,18},{14,20},{16,22},{... | collective-permute-start | bytes 49160 | tf_op jit(solution)/shard_map/ppermute | solution.py:368
  5.8 3.0 %collective-permute-start.2 = (f32[4,1024]{1,0:T(4,128)S(1)}, f32[4,1024]{1,0:T(4,128)S(1)}, u32[]{:S(2)}, u32[]{:S(2)}) collective-permute-start(f32[4,1024]{1,0:T(4,128)S(1)} %get-tuple-element.37.own), channel_id=1, source_target_pairs={{0,4},{2,6},{4,8},{6,10},{8,12},{10,14},{12,16},{14,18},{16,20},{1... | collective-permute-start | bytes 49160 | tf_op jit(solution)/shard_map/ppermute | solution.py:368
  7.0 3.5 %collective-permute-start.1 = (f32[4,1024]{1,0:T(4,128)S(1)}, f32[4,1024]{1,0:T(4,128)S(1)}, u32[]{:S(2)}, u32[]{:S(2)}) collective-permute-start(f32[4,1024]{1,0:T(4,128)S(1)} %get-tuple-element.37.own), channel_id=1, source_target_pairs={{0,2},{2,4},{4,6},{6,8},{8,10},{10,12},{12,14},{14,16},{16,18},{18... | collective-permute-start | bytes 49160 | tf_op jit(solution)/shard_map/ppermute | solution.py:368
  7.0 3.5 %copy-start.5 = (bf16[1,512,1024]{2,1,0:T(8,128)(2,1)S(1)}, bf16[1,512,1024]{2,1,0:T(8,128)(2,1)}, u32[]{:S(2)}) copy-start(bf16[1,512,1024]{2,1,0:T(8,128)(2,1)} %param.22) | copy-start | bytes 3145732
  16.4 6.5 %collective-permute-start.5 = (bf16[512,1024]{1,0:T(8,128)(2,1)S(1)}, bf16[512,1024]{1,0:T(8,128)(2,1)S(1)}, u32[]{:S(2)}, u32[]{:S(2)}) collective-permute-start(bf16[512,1024]{1,0:T(8,128)(2,1)S(1)} %get-tuple-element.41), channel_id=1, source_target_pairs={{0,1},{1,0},{2,3},{3,2},{4,5},{5,4},{6,7},{7,6},{8,9},{9,8},{10,11... | collective-permute-start | bytes 3145736 | tf_op jit(solution)/shard_map/ppermute | solution.py:330
  18.4 2.9 %copy-start = (f32[1,512,1024]{2,1,0:T(8,128)S(1)}, f32[1,512,1024]{2,1,0:T(8,128)}, u32[]{:S(2)}) copy-start(f32[1,512,1024]{2,1,0:T(8,128)} %param.24) | copy-start | bytes 6291460
  18.4 2.9 %copy-start.1 = (f32[1,512,1024]{2,1,0:T(8,128)S(1)}, f32[1,512,1024]{2,1,0:T(8,128)}, u32[]{:S(2)}) copy-start(f32[1,512,1024]{2,1,0:T(8,128)} %param.19) | copy-start | bytes 6291460
  21.3 1.6 %collective-permute-start.6 = (f32[24,1024]{1,0:T(8,128)S(1)}, f32[24,1024]{1,0:T(8,128)S(1)}, u32[]{:S(2)}, u32[]{:S(2)}) collective-permute-start(f32[24,1024]{1,0:T(8,128)S(1)} %first_gradients.1.refs_3_), channel_id=1, source_target_pairs={{0,1},{1,0},{2,3},{3,2},{4,5},{5,4},{6,7},{7,6},{8,9},{9,8},{10,11... | collective-permute-start | bytes 294920 | tf_op jit(solution)/shard_map/ppermute | solution.py:330
  21.3 1.6 %copy-start.2 = (f32[1,16,1024]{2,1,0:T(8,128)S(1)}, f32[1,16,1024]{2,1,0:T(8,128)}, u32[]{:S(2)}) copy-start(f32[1,16,1024]{2,1,0:T(8,128)} %param.23) | copy-start | bytes 196612
  21.3 1.6 %copy-start.3 = (f32[1,16,1024]{2,1,0:T(8,128)S(1)}, f32[1,16,1024]{2,1,0:T(8,128)}, u32[]{:S(2)}) copy-start(f32[1,16,1024]{2,1,0:T(8,128)} %param.18) | copy-start | bytes 196612
  21.3 1.6 %copy-start.4 = (f32[1,3,1024]{2,0,1:T(1,128)S(1)}, f32[1,3,1024]{2,0,1:T(1,128)}, u32[]{:S(2)}) copy-start(f32[1,3,1024]{2,0,1:T(1,128)} %param.25) | copy-start | bytes 36868
